TPU v7x, 512 devices: a whole 4x8x8 slice. The times are simulated.
512 devices in a mesh: section: 8 (over x, y_hi), seq: 64 (over y_lo, z, core).
Axes of the slice: x: 4, y: 8 (y_hi: 2, y_lo: 4; y = y_hi * 4 + y_lo), z: 8, core: 2. Of those that a mesh axis runs over, the one named last changes fastest.
Arguments:
- hidden: bfloat16 [8, 2, 4096, 2048], P('section', None, 'seq'), may hold values from -16 to 16
- queries: bfloat16 [8, 2, 4096, 1024], P('section', None, 'seq'), may hold values from -6 to 6
- keys_values: bfloat16 [8, 2, 4096, 512], P('section', None, 'seq'), may hold values from -6 to 6
- out_grad: bfloat16 [8, 2, 4096, 2048], P('section', None, 'seq'), may hold values from -96 to 96
- qkv_weight: bfloat16 [8, 2048, 1536], P('section', 'seq'), may hold values from -0.125 to 0.125
- out_weight: bfloat16 [8, 2048, 1024], P('section', 'seq'), may hold values from -0.1875 to 0.1875
- adapter_down_maps: bfloat16 [8, 2048, 128], P('section', 'seq'), may hold values from -0.125 to 0.125
- adapter_up_maps: bfloat16 [8, 64, 1280], P('section'), may hold values from -0.119628906 to 0.119628906
Outputs:
- passed_grad: bfloat16 [8, 2, 4096, 2048], P('section', None, 'seq')
- a_grad: float32 [8, 2048, 128], P('section', 'seq')
- b_grad: float32 [8, 64, 1280], P('section', None, 'seq')
All inputs are finite; a program needn't handle non-finite values.
Results may differ from a plain program's by a relative error of at most 0.0071.
Values may be sent and summed in bfloat16 or wider, within the bound.
No kernel may reach another device: no remote copies, remote signals or barrier semaphores. Data moves between devices by JAX's collectives and lax.ppermute only.
A program may use at most 64 MiB of HBM per device.

v0:
```python
import jax
import jax.numpy as jnp
from jax import lax
from jax.sharding import PartitionSpec as P

MODEL_WIDTH = 2048
QUERY_HEADS = 16
KEY_VALUE_HEADS = 4
HEAD_SIZE = 64
ADAPTER_RANK = 64
ADAPTER_NUMER = 128
GRADIENT_SCALE = 32
SEQS = 2


def from_behind(block, axis, distance):
    devices = range(lax.axis_size(axis))
    route = [((i - distance) % len(devices), i) for i in devices]
    return lax.ppermute(block, axis, route)


def attend(query_rows, grad_rows, key_rows, query_pos):
    score_scale = HEAD_SIZE ** (-0.5)
    row_count = query_rows.shape[0]
    col_count = key_rows.shape[0]
    group_q = query_rows.shape[1] // HEAD_SIZE
    row_size = row_count // 4
    col_size = col_count // 4
    key_pos = jnp.arange(col_count)
    tile_first = jnp.array([first for first in range(4) for second in range(first + 1)], jnp.int32)
    tile_second = jnp.array(
        [second for first in range(4) for second in range(first + 1)], jnp.int32
    )

    def score_tile(row_tile, col_tile):
        query_tile = lax.dynamic_slice_in_dim(query_rows, row_tile * row_size, row_size, 0).reshape(
            row_size, group_q, HEAD_SIZE
        )
        grad_tile = lax.dynamic_slice_in_dim(grad_rows, row_tile * row_size, row_size, 0).reshape(
            row_size, group_q, HEAD_SIZE
        )
        pair_tile = lax.dynamic_slice_in_dim(key_rows, col_tile * col_size, col_size, 0)
        key_tile = pair_tile[:, :HEAD_SIZE]
        value_tile = pair_tile[:, HEAD_SIZE:]
        scores = (
            jnp.einsum("qhd,kd->qhk", query_tile, key_tile, preferred_element_type=jnp.float32)
            * score_scale
        )
        row_place = lax.dynamic_slice_in_dim(query_pos, row_tile * row_size, row_size, 0)
        col_place = lax.dynamic_slice_in_dim(key_pos, col_tile * col_size, col_size, 0)
        allowed = row_place[:, None, None] >= col_place[None, None, :]
        scores = jnp.where(allowed, scores, -jnp.inf)
        prob_grad = jnp.einsum(
            "qhd,kd->qhk", grad_tile, value_tile, preferred_element_type=jnp.float32
        )
        return (query_tile, grad_tile, key_tile, scores, prob_grad)

    def row_stats(state, tiles):
        row_max, row_total, weighted = state
        row_tile, col_tile = tiles
        scores, prob_grad = score_tile(row_tile, col_tile)[3:]
        row_start = row_tile * row_size
        old_max = lax.dynamic_slice_in_dim(row_max, row_start, row_size, 0)
        old_total = lax.dynamic_slice_in_dim(row_total, row_start, row_size, 0)
        old_weighted = lax.dynamic_slice_in_dim(weighted, row_start, row_size, 0)
        new_max = jnp.maximum(old_max, jnp.max(scores, axis=2))
        shrink = jnp.exp(old_max - new_max)
        exponent = jnp.exp(scores - new_max[:, :, None])
        new_total = old_total * shrink + jnp.sum(exponent, axis=2)
        new_weighted = old_weighted * shrink + jnp.sum(exponent * prob_grad, axis=2)
        row_max = lax.dynamic_update_slice_in_dim(row_max, new_max, row_start, 0)
        row_total = lax.dynamic_update_slice_in_dim(row_total, new_total, row_start, 0)
        weighted = lax.dynamic_update_slice_in_dim(weighted, new_weighted, row_start, 0)
        return ((row_max, row_total, weighted), None)

    start_state = (
        jnp.full((row_count, group_q), -jnp.inf, jnp.float32),
        jnp.zeros((row_count, group_q), jnp.float32),
        jnp.zeros((row_count, group_q), jnp.float32),
    )
    (row_max, row_total, weighted), unused = lax.scan(
        row_stats, start_state, (tile_first, tile_second)
    )
    row_delta = weighted / row_total

    def tile_grads(state, tiles):
        query_sum, key_sum, value_sum = state
        row_tile, col_tile = tiles
        query_tile, grad_tile, key_tile, scores, prob_grad = score_tile(row_tile, col_tile)
        row_start = row_tile * row_size
        col_start = col_tile * col_size
        tile_max = lax.dynamic_slice_in_dim(row_max, row_start, row_size, 0)
        tile_total = lax.dynamic_slice_in_dim(row_total, row_start, row_size, 0)
        tile_delta = lax.dynamic_slice_in_dim(row_delta, row_start, row_size, 0)
        attn_prob = jnp.exp(scores - tile_max[:, :, None]) / tile_total[:, :, None]
        score_grad = (attn_prob * (prob_grad - tile_delta[:, :, None]) * score_scale).astype(
            jnp.bfloat16
        )
        prob_half = attn_prob.astype(jnp.bfloat16)
        query_part = jnp.einsum(
            "qhk,kd->qhd", score_grad, key_tile, preferred_element_type=jnp.float32
        ).reshape(row_size, group_q * HEAD_SIZE)
        key_part = jnp.einsum(
            "qhk,qhd->kd", score_grad, query_tile, preferred_element_type=jnp.float32
        )
        value_part = jnp.einsum(
            "qhk,qhd->kd", prob_half, grad_tile, preferred_element_type=jnp.float32
        )
        query_sum = lax.dynamic_update_slice_in_dim(
            query_sum,
            lax.dynamic_slice_in_dim(query_sum, row_start, row_size, 0) + query_part,
            row_start,
            0,
        )
        key_sum = lax.dynamic_update_slice_in_dim(
            key_sum,
            lax.dynamic_slice_in_dim(key_sum, col_start, col_size, 0) + key_part,
            col_start,
            0,
        )
        value_sum = lax.dynamic_update_slice_in_dim(
            value_sum,
            lax.dynamic_slice_in_dim(value_sum, col_start, col_size, 0) + value_part,
            col_start,
            0,
        )
        return ((query_sum, key_sum, value_sum), None)

    grad_state = (
        jnp.zeros((row_count, group_q * HEAD_SIZE), jnp.float32),
        jnp.zeros((col_count, HEAD_SIZE), jnp.float32),
        jnp.zeros((col_count, HEAD_SIZE), jnp.float32),
    )
    (query_sum, key_sum, value_sum), unused = lax.scan(
        tile_grads, grad_state, (tile_first, tile_second)
    )
    return (query_sum.astype(jnp.bfloat16), jnp.concatenate([key_sum, value_sum], axis=1))


def per_device(
    hidden,
    queries,
    keys_values,
    out_grad,
    qkv_weight,
    out_weight,
    adapter_down_maps,
    adapter_up_maps,
):
    devices = lax.axis_size("seq")
    own_index = lax.axis_index("seq")
    query_parts = devices // (KEY_VALUE_HEADS * SEQS)
    per_seq = hidden.shape[2]
    per_part = per_seq // query_parts
    kv_cols = 2 * HEAD_SIZE
    group_width = QUERY_HEADS // KEY_VALUE_HEADS * HEAD_SIZE
    tokens_here = SEQS * per_seq
    q_cols = QUERY_HEADS * HEAD_SIZE
    hidden_rows = hidden[0].reshape(tokens_here, MODEL_WIDTH)
    query_send = (
        queries[0]
        .reshape(SEQS, query_parts, per_part, KEY_VALUE_HEADS, group_width)
        .transpose(3, 0, 1, 2, 4)
        .reshape(devices, per_part, group_width)
    )
    kv_local = keys_values[0].reshape(SEQS, per_seq, KEY_VALUE_HEADS, kv_cols).transpose(2, 0, 1, 3)
    kv_send = jnp.broadcast_to(
        kv_local[:, :, None], (KEY_VALUE_HEADS, SEQS, query_parts, per_seq, kv_cols)
    ).reshape(devices, per_seq, kv_cols)
    weight_all, output_all, down_all = (
        lax.all_gather(qkv_weight[0], "seq", axis=0, tiled=True),
        lax.all_gather(out_weight[0], "seq", axis=0, tiled=True),
        lax.all_gather(adapter_down_maps[0], "seq", axis=0, tiled=True),
    )
    attn_grad = jnp.dot(
        out_grad[0].reshape(tokens_here, MODEL_WIDTH),
        output_all,
        preferred_element_type=jnp.float32,
    ).astype(jnp.bfloat16)
    grad_send = (
        attn_grad.reshape(SEQS, query_parts, per_part, KEY_VALUE_HEADS, group_width)
        .transpose(3, 0, 1, 2, 4)
        .reshape(devices, per_part, group_width)
    )
    query_in, grad_in, kv_in = (
        lax.all_to_all(query_send, "seq", split_axis=0, concat_axis=0, tiled=True),
        lax.all_to_all(grad_send, "seq", split_axis=0, concat_axis=0, tiled=True),
        lax.all_to_all(kv_send, "seq", split_axis=0, concat_axis=0, tiled=True),
    )
    grad_rows = grad_in.reshape(devices * per_part, group_width)
    query_rows = query_in.reshape(devices * per_part, group_width)
    key_rows = kv_in.reshape(devices * per_seq, kv_cols)
    own_part = own_index % query_parts
    row_ids = jnp.arange(devices * per_part)
    query_pos = row_ids // per_part * per_seq + own_part * per_part + row_ids % per_part
    query_gradient, kv_grad = attend(query_rows, grad_rows, key_rows, query_pos)
    query_back, kv_back = (
        lax.all_to_all(
            query_gradient.reshape(devices, per_part, group_width).astype(jnp.float32),
            "seq",
            split_axis=0,
            concat_axis=0,
            tiled=True,
        ).astype(jnp.bfloat16),
        lax.all_to_all(
            kv_grad.reshape(devices, per_seq, kv_cols),
            "seq",
            split_axis=0,
            concat_axis=0,
            tiled=True,
        ),
    )
    query_local = (
        query_back.reshape(KEY_VALUE_HEADS, SEQS, query_parts, per_part, group_width)
        .transpose(1, 2, 3, 0, 4)
        .reshape(tokens_here, q_cols)
    )
    kv_local_grad = jnp.sum(
        kv_back.reshape(KEY_VALUE_HEADS, SEQS, query_parts, per_seq, kv_cols), axis=2
    ).astype(jnp.bfloat16)
    key_local = (
        kv_local_grad[..., :HEAD_SIZE]
        .transpose(1, 2, 0, 3)
        .reshape(tokens_here, KEY_VALUE_HEADS * HEAD_SIZE)
    )
    value_local = (
        kv_local_grad[..., HEAD_SIZE:]
        .transpose(1, 2, 0, 3)
        .reshape(tokens_here, KEY_VALUE_HEADS * HEAD_SIZE)
    )
    up_maps = adapter_up_maps[0]
    adapter_between = jnp.concatenate(
        [
            lax.dot_general(
                query_local,
                up_maps[:, :q_cols],
                (((1,), (1,)), ((), ())),
                preferred_element_type=jnp.float32,
            ),
            lax.dot_general(
                value_local,
                up_maps[:, q_cols:],
                (((1,), (1,)), ((), ())),
                preferred_element_type=jnp.float32,
            ),
        ],
        axis=1,
    ).astype(jnp.bfloat16)
    grad_qkv = jnp.concatenate([query_local, key_local, value_local], axis=1)
    adapter_scale = ADAPTER_NUMER / ADAPTER_RANK
    input_gradient = lax.dot_general(
        grad_qkv, weight_all, (((1,), (1,)), ((), ())), preferred_element_type=jnp.float32
    )
    input_gradient = input_gradient + adapter_scale * lax.dot_general(
        adapter_between, down_all, (((1,), (1,)), ((), ())), preferred_element_type=jnp.float32
    )
    input_gradient = input_gradient.astype(jnp.bfloat16).reshape(1, SEQS, per_seq, MODEL_WIDTH)
    passed = from_behind(input_gradient, "section", -1)
    adapter_reduced = jnp.dot(hidden_rows, down_all, preferred_element_type=jnp.float32).astype(
        jnp.bfloat16
    )
    scale_factor = adapter_scale / GRADIENT_SCALE
    a_term = scale_factor * lax.dot_general(
        hidden_rows, adapter_between, (((0,), (0,)), ((), ())), preferred_element_type=jnp.float32
    )
    b_term = scale_factor * jnp.concatenate(
        [
            lax.dot_general(
                adapter_reduced[:, :ADAPTER_RANK],
                query_local,
                (((0,), (0,)), ((), ())),
                preferred_element_type=jnp.float32,
            ),
            lax.dot_general(
                adapter_reduced[:, ADAPTER_RANK:],
                value_local,
                (((0,), (0,)), ((), ())),
                preferred_element_type=jnp.float32,
            ),
        ],
        axis=1,
    )
    a_sum, b_sum = (
        lax.psum_scatter(a_term, "seq", scatter_dimension=0, tiled=True),
        lax.psum_scatter(b_term, "seq", scatter_dimension=1, tiled=True),
    )
    return (passed, a_sum[None], b_sum[None])


def solution(mesh):
    return jax.shard_map(
        per_device,
        mesh=mesh,
        in_specs=(
            P("section", None, "seq", None),
            P("section", None, "seq", None),
            P("section", None, "seq", None),
            P("section", None, "seq", None),
            P("section", "seq", None),
            P("section", "seq", None),
            P("section", "seq", None),
            P("section", None, None),
        ),
        out_specs=(
            P("section", None, "seq", None),
            P("section", "seq", None),
            P("section", None, "seq"),
        ),
        check_vma=False,
    )
```

profile of v0, /device:TPU:6, one launch (start us, length us, event | category | flops | bytes accessed | tf_op | source)
XLA Modules:
  0.0 1317.5 jit_solution(9286400375090018198)
XLA Ops:
  9.6 14.5 %all-to-all-start = ((bf16[64,8,256]{2,1,0:T(8,128)(2,1)}), bf16[64,8,256]{2,1,0:T(8,128)(2,1)S(1)}, u32[]{:S(2)}, u32[]{:S(2)}) async-start(bf16[64,8,256]{2,1,0:T(8,128)(2,1)} %bitcast.2), calls=%async_computation | async-start | bytes 524288 | tf_op jit(solution)/shard_map/all_to_all | solution.py:186
  25.1 11.5 all-to-all-done
  37.8 5.8 all-to-all-start.1
  43.6 106.8 %all-gather.6.cloned.1.call-done = bf16[1,2048,1024]{2,1,0:T(8,128)(2,1)} async-done(((bf16[1,32,1024]{2,1,0:T(8,128)(2,1)}), bf16[1,2048,1024]{2,1,0:T(8,128)(2,1)}) %all-gather.6.cloned.1.call-update) | async-done | bytes 4194320 | tf_op jit(solution)/shard_map/all_gather | solution.py:172
  150.4 2.9 fusion.24
  154.0 7.0 all-to-all-start.2
  163.4 10.2 all-to-all-done.2
  173.8 66.2 %while.30 = (s32[]{:T(128)}, f32[512,4]{0,1:T(4,128)S(1)}, f32[512,4]{0,1:T(4,128)S(1)}, f32[512,4]{0,1:T(4,128)S(1)}, s32[512]{0:T(512)S(1)}, /*index=5*/s32[40...) while((s32[]{:T(128)}, f32[512,4]{0,1:T(4,128)S(1)}, ...), condition=%wide.region_4.5_spmd.clone, body=%wide.region_0.4_spmd.sunk.clone.sunk | while | flops 140641792 | bytes 7552837 | solution.py:81
  243.0 129.9 %while.31 = (s32[]{:T(128)}, f32[512,256]{1,0:T(8,128)}, f32[4096,64]{0,1:T(8,128)}, f32[4096,64]{0,1:T(8,128)}, s32[512]{0:T(512)S(1)}, /*index=5*/s32[4096]{0:...) while((s32[]{:T(128)}, f32[512,256]{1,0:T(8,128)}, ...), condition=%wide.region_6.7_spmd.clone, body=%wide.region_5.6_spmd.sunk.clone.sunk | while | flops 340557824 | bytes 15368105 | solution.py:134
  254.0 2.0 fusion.96
  267.0 2.0 fusion.96
  274.9 2.0 fusion.95
  280.0 2.0 fusion.96
  293.0 2.0 fusion.96
  306.0 2.0 fusion.96
  319.0 2.0 fusion.96
  331.9 2.0 fusion.96
  339.8 2.0 fusion.95
  344.9 2.0 fusion.96
  357.9 2.0 fusion.96
  365.8 2.0 fusion.95
  370.9 2.0 fusion.96
  374.8 5.1 all-to-all-start.3
  380.0 3.2 copy.58
  385.2 4.2 pad_maximum_fusion
  389.4 3.1 all-to-all-done.3
  392.5 7.8 all-to-all-start.4
  400.3 121.4 %all-gather.2 = bf16[1,2048,128]{2,1,0:T(8,128)(2,1)S(1)} all-gather(bf16[1,32,128]{2,1,0:T(8,128)(2,1)S(1)} %copy-done.6), channel_id=4, replica_groups=mesh['section'=8,'seq'=64] {'seq'}, dimensions={1}, use_global_device_ids=true | all-gather | bytes 532480 | tf_op jit(solution)/shard_map/all_gather | solution.py:173
  528.7 4.9 fusion.17
  533.9 10.7 collective-permute-start
  546.6 481.5 %all-reduce.3.cloned.1.call-done = f32[64,1280]{1,0:T(8,128)} async-done(((f32[64,1280]{1,0:T(8,128)}), f32[64,1280]{1,0:T(8,128)}) %all-reduce.3.cloned.1.call-update) | async-done | bytes 327696
  1029.7 279.0 %reduce-scatter.5.cloned.1.call-done = f32[32,128]{1,0:T(8,128)} async-done(((f32[2048,128]{1,0:T(8,128)}), f32[32,128]{1,0:T(8,128)}) %reduce-scatter.5.cloned.1.call-update) | async-done | bytes 16400
  (406 shorter events, 169.5 us)
Async XLA Ops:
  7.2 514.5 %copy-start = (bf16[1,2,64,2048]{3,2,1,0:T(8,128)(2,1)S(1)}, bf16[1,2,64,2048]{3,2,1,0:T(8,128)(2,1)}, u32[]{:S(2)}) copy-start(bf16[1,2,64,2048]{3,2,1,0:T(8,128)(2,1)} %param.14) | copy-start | bytes 1572868
  7.2 143.2 %all-gather.6.cloned.1.call-start = ((), (), s32[]{:S(2)}) async-start(), calls=%async_computation.6 | async-start | bytes 4259840 | tf_op jit(solution)/shard_map/all_gather | solution.py:172
  9.6 140.8 %copy-start.4 = (bf16[1,2,64,2048]{3,2,1,0:T(8,128)(2,1)S(1)}, bf16[1,2,64,2048]{3,2,1,0:T(8,128)(2,1)}, u32[]{:S(2)}) copy-start(bf16[1,2,64,2048]{3,2,1,0:T(8,128)(2,1)} %param.17) | copy-start | bytes 1572868
  9.6 27.0 %all-to-all-start = ((bf16[64,8,256]{2,1,0:T(8,128)(2,1)}), bf16[64,8,256]{2,1,0:T(8,128)(2,1)S(1)}, u32[]{:S(2)}, u32[]{:S(2)}) async-start(bf16[64,8,256]{2,1,0:T(8,128)(2,1)} %bitcast.2), calls=%async_computation | async-start | bytes 524288 | tf_op jit(solution)/shard_map/all_to_all | solution.py:186
  37.8 116.2 %all-to-all-start.1 = ((bf16[64,64,128]{2,1,0:T(8,128)(2,1)}), bf16[64,64,128]{2,1,0:T(8,128)(2,1)S(1)}, u32[]{:S(2)}, u32[]{:S(2)}) async-start(bf16[64,64,128]{2,1,0:T(8,128)(2,1)} %bitcast.5), calls=%async_computation.1 | async-start | bytes 2097152 | tf_op jit(solution)/shard_map/all_to_all | solution.py:188
  153.3 20.5 %copy-start.7 = (s32[10]{0:T(128)S(1)}, s32[10]{0:T(128)}, u32[]{:S(2)}) copy-start(s32[10]{0:T(128)} %constant.102.clone..sunk.4) | copy-start | bytes 124
  153.3 20.5 %copy-start.8 = (s32[10]{0:T(128)S(1)}, s32[10]{0:T(128)}, u32[]{:S(2)}) copy-start(s32[10]{0:T(128)} %constant.103.clone..sunk.4) | copy-start | bytes 124
  154.0 19.5 %all-to-all-start.2 = ((bf16[64,8,256]{2,1,0:T(8,128)(2,1)}), bf16[64,8,256]{2,1,0:T(8,128)(2,1)S(1)}, u32[]{:S(2)}, u32[]{:S(2)}) async-start(bf16[64,8,256]{2,1,0:T(8,128)(2,1)} %bitcast.11), calls=%async_computation.2 | async-start | bytes 524288 | tf_op jit(solution)/shard_map/all_to_all | solution.py:187
  161.1 367.6 %all-gather.8.cloned.1.call-start = ((), (), s32[]{:S(2)}) async-start(), calls=%async_computation.7 | async-start | bytes 6389760 | tf_op jit(solution)/shard_map/all_gather | solution.py:171
  243.0 4.5 copy-start.2
  256.0 4.5 copy-start.2
  269.0 4.5 copy-start.2
  280.0 2.0 copy-start.3
  282.0 4.5 copy-start.2
  295.0 4.5 copy-start.2
  308.0 4.5 copy-start.2
  319.0 2.0 copy-start.3
  321.0 4.5 copy-start.2
  333.9 4.5 copy-start.2
  344.9 2.0 copy-start.3
  346.9 4.5 copy-start.2
  357.9 2.0 copy-start.3
  359.9 4.5 copy-start.2
  370.9 2.0 copy-start.3
  373.0 10.2 copy-start.1
  374.8 17.6 %all-to-all-start.3 = ((bf16[64,8,256]{2,1,0:T(8,128)(2,1)}), bf16[64,8,256]{2,1,0:T(8,128)(2,1)S(1)}, u32[]{:S(2)}, u32[]{:S(2)}) async-start(bf16[64,8,256]{2,1,0:T(8,128)(2,1)} %bitcast_convert_fusion), calls=%async_computation.3 | async-start | bytes 524288 | tf_op jit(solution)/shard_map/all_to_all | solution.py:198
  392.5 7.8 copy-start.6
  392.5 130.9 %all-to-all-start.4 = ((f32[64,64,128]{2,1,0:T(8,128)}), f32[64,64,128]{2,1,0:T(8,128)S(1)}, u32[]{:S(2)}, u32[]{:S(2)}) async-start(f32[64,64,128]{2,1,0:T(8,128)} %bitcast.16), calls=%async_computation.4 | async-start | bytes 4194304 | tf_op jit(solution)/shard_map/all_to_all | solution.py:205
  400.3 627.8 %all-reduce.3.cloned.1.call-start = ((), (), s32[]{:S(2)}) async-start(), calls=%async_computation.9 | async-start | bytes 655360
  400.3 122.0 %copy-start.5 = (bf16[1,64,1280]{2,1,0:T(8,128)(2,1)S(1)}, bf16[1,64,1280]{2,1,0:T(8,128)(2,1)}, u32[]{:S(2)}) copy-start(bf16[1,64,1280]{2,1,0:T(8,128)(2,1)} %param.21) | copy-start | bytes 491524
  525.8 782.9 %reduce-scatter.5.cloned.1.call-start = ((), (), s32[]{:S(2)}) async-start(), calls=%async_computation.8 | async-start | bytes 1064960
  533.9 495.8 %collective-permute-start = (bf16[1,2,64,2048]{3,2,1,0:T(8,128)(2,1)S(1)}, bf16[1,2,64,2048]{3,2,1,0:T(8,128)(2,1)S(1)}, u32[]{:S(2)}, u32[]{:S(2)}) collective-permute-start(bf16[1,2,64,2048]{3,2,1,0:T(8,128)(2,1)S(1)} %bitcast.175), channel_id=1, source_target_pairs={{64,0},{128,64},{192,128},{256,192},{320,256},{384,320},{448,384},... | collective-permute-start | bytes 1572872 | tf_op jit(solution)/shard_map/ppermute | solution.py:19
  (5 other events, 9.9 us)
Sparse Core Ops, SparseCore 0:
  10.2 140.1 all-gather.5
  164.1 125.5 all-gather.7
  525.9 502.1 all-reduce.2
  1031.0 277.6 reduce-scatter.4
where the time goes:
time: 1320 us
  waiting for transfers between devices  894 us (68%)
  matrix products  126 us (10%)
  blocking collectives  121 us (9%)
  local copies, waits for them, and re-layouts  65.7 us (5%)
  starting transfers between devices  51.1 us (4%)
  loops' own time  27.8 us (2%)
  other arithmetic  17 us (1%)
  between operations  14.7 us (1%)
    unnamed x6, waiting for transfers between devices  762 us
    all_gather x1, blocking collectives, per_device(): lax.all_gather(adapter_down_maps[0], 'seq', axis=0, tiled=True)  121 us
    all_gather x1, waiting for transfers between devices, per_device(): lax.all_gather(out_weight[0], 'seq', axis=0, tiled=True)  107 us
    dot_general x20, matrix products, score_tile(): jnp.einsum('qhd,kd->qhk', query_tile, key_tile, preferred_element_type=jn...  31.7 us
    dot_general x20, matrix products, score_tile(): jnp.einsum('qhd,kd->qhk', grad_tile, value_tile, preferred_element_type=j...  30.7 us
  transfers between devices with their start and end apart: 10, of which 6 were waited for; matrix products, arithmetic and copies ran while one was open for 16% of the time, Pallas kernels for 0%

commit v1 on v0

v1 whole, which is shorter than its diff:
```python
import jax
import jax.numpy as jnp
from jax import lax
from jax.experimental import pallas as pl
from jax.experimental.pallas import tpu as pltpu
from jax.sharding import Mesh, PartitionSpec as P

MODEL_WIDTH = 2048
QUERY_HEADS = 16
KEY_VALUE_HEADS = 4
HEAD_SIZE = 64
ADAPTER_RANK = 64
ADAPTER_NUMER = 128
GRADIENT_SCALE = 32
SEQS = 2
LEN = 4096

LINE = 4
RING = 8
CORES = 2
SEQ_AXES = ("y", "z", "core")
DEVICES = LINE * RING * CORES
PER_SEQ = LEN // DEVICES
Q_COLS = QUERY_HEADS * HEAD_SIZE
KV_COLS = 2 * HEAD_SIZE
GROUP = QUERY_HEADS // KEY_VALUE_HEADS
GROUP_WIDTH = GROUP * HEAD_SIZE
PAIR_WIDTH = CORES * GROUP_WIDTH

CHUNK = CORES * PER_SEQ
SPAN = RING * CHUNK
COLS = GROUP * CHUNK
TILE = SPAN
TILES = LEN // TILE
EXP_SCALE = HEAD_SIZE ** (-0.5) * 1.4426950408889634


def dot(a, b):
    return jnp.dot(a, b, preferred_element_type=jnp.float32)


def head_columns(rows):
    turned = rows.astype(jnp.float32).T
    return jnp.concatenate(
        [turned[h * HEAD_SIZE : (h + 1) * HEAD_SIZE] for h in range(GROUP)], axis=1
    )


def causal(scores, first_key, first_row):
    key_pos = first_key + lax.broadcasted_iota(jnp.int32, scores.shape, 0)
    row_pos = first_row + lax.broadcasted_iota(jnp.int32, scores.shape, 1) % CHUNK
    return jnp.where(row_pos >= key_pos, scores, -jnp.inf)


def forward_kernel(part_ref, query_ref, kv_ref, turned_ref, out_ref, log_ref):
    part = part_ref[0]

    def chunk(j, carry):
        first_row = j * SPAN + part * CHUNK
        columns = head_columns(query_ref[j])
        query_cols = jnp.concatenate([columns, jnp.zeros_like(columns)], axis=0).astype(
            jnp.bfloat16
        )

        def tile(t, state, masked):
            top, total, mixed = state
            scores = dot(kv_ref[t], query_cols)
            if masked:
                scores = causal(scores, t * TILE, first_row)
            new_top = jnp.maximum(top, jnp.max(scores, axis=0, keepdims=True))
            shrink = jnp.exp2((top - new_top) * EXP_SCALE)
            power = jnp.exp2(scores * EXP_SCALE - new_top * EXP_SCALE)
            total = total * shrink + jnp.sum(power, axis=0, keepdims=True)
            mixed = mixed * shrink + dot(turned_ref[t, HEAD_SIZE:], power.astype(jnp.bfloat16))
            return new_top, total, mixed

        state = (
            jnp.full((1, COLS), -jnp.inf, jnp.float32),
            jnp.zeros((1, COLS), jnp.float32),
            jnp.zeros((HEAD_SIZE, COLS), jnp.float32),
        )
        last = first_row // TILE
        state = lax.fori_loop(0, last, lambda t, s: tile(t, s, False), state)
        top, total, mixed = tile(last, state, True)
        out_ref[j] = mixed / total
        log_ref[j] = top * EXP_SCALE + jnp.log2(total)
        return carry

    lax.fori_loop(0, LINE, chunk, 0)


def backward_kernel(
    part_ref, query_ref, grad_ref, kv_ref, turned_ref, out_ref, log_ref, dq_ref, dkv_ref, acc_ref
):
    part = part_ref[0]
    scale = HEAD_SIZE ** (-0.5)
    acc_ref[...] = jnp.zeros_like(acc_ref)

    def chunk(j, carry):
        first_row = j * SPAN + part * CHUNK
        query_half = head_columns(query_ref[j])
        grad_half = head_columns(grad_ref[j])
        blank = jnp.zeros_like(query_half)
        query_full = jnp.concatenate([query_half, blank], axis=0)
        grad_full = jnp.concatenate([blank, grad_half], axis=0)
        query_cols = query_full.astype(jnp.bfloat16)
        grad_cols = grad_full.astype(jnp.bfloat16)
        query_rows = query_full.T.astype(jnp.bfloat16)
        grad_rows = grad_full.T.astype(jnp.bfloat16)
        delta = jnp.sum(grad_half * out_ref[j], axis=0, keepdims=True)
        log_total = log_ref[j]

        def tile(t, query_sum, masked):
            pair = kv_ref[t]
            scores = dot(pair, query_cols)
            if masked:
                scores = causal(scores, t * TILE, first_row)
            prob = jnp.exp2(scores * EXP_SCALE - log_total)
            prob_grad = dot(pair, grad_cols)
            score_grad = (prob * (prob_grad - delta)).astype(jnp.bfloat16)
            acc_ref[t] += dot(score_grad, query_rows) + dot(prob.astype(jnp.bfloat16), grad_rows)
            return query_sum + dot(turned_ref[t, :HEAD_SIZE], score_grad)

        last = first_row // TILE
        query_sum = lax.fori_loop(
            0, last, lambda t, s: tile(t, s, False), jnp.zeros((HEAD_SIZE, COLS), jnp.float32)
        )
        query_sum = tile(last, query_sum, True) * scale
        stacked = jnp.concatenate(
            [query_sum[:, h * CHUNK : (h + 1) * CHUNK] for h in range(GROUP)], axis=0
        )
        dq_ref[j] = stacked.T.astype(jnp.bfloat16)
        return carry

    lax.fori_loop(0, LINE, chunk, 0)
    lane = lax.broadcasted_iota(jnp.int32, acc_ref.shape, 2)
    dkv_ref[...] = (acc_ref[...] * jnp.where(lane < HEAD_SIZE, scale, 1.0)).astype(jnp.bfloat16)


VMEM = pl.BlockSpec(memory_space=pltpu.VMEM)
SMEM = pl.BlockSpec(memory_space=pltpu.SMEM)
PARAMS = pltpu.CompilerParams(vmem_limit_bytes=48 * 2**20)


def attend_forward(part, query, kv, turned):
    return pl.pallas_call(
        forward_kernel,
        out_shape=(
            jax.ShapeDtypeStruct((LINE, HEAD_SIZE, COLS), jnp.float32),
            jax.ShapeDtypeStruct((LINE, 1, COLS), jnp.float32),
        ),
        in_specs=[SMEM, VMEM, VMEM, VMEM],
        out_specs=(VMEM, VMEM),
        compiler_params=PARAMS,
        name="attention_forward",
    )(part, query, kv, turned)


def attend_backward(part, query, grad, kv, turned, out, log_total):
    return pl.pallas_call(
        backward_kernel,
        out_shape=(
            jax.ShapeDtypeStruct((LINE, CHUNK, GROUP_WIDTH), jnp.bfloat16),
            jax.ShapeDtypeStruct((TILES, TILE, KV_COLS), jnp.bfloat16),
        ),
        in_specs=[SMEM] + [VMEM] * 6,
        out_specs=(VMEM, VMEM),
        scratch_shapes=[pltpu.VMEM((TILES, TILE, KV_COLS), jnp.float32)],
        compiler_params=PARAMS,
        name="attention_backward",
    )(part, query, grad, kv, turned, out, log_total)


def exchange(blocks, axes):
    return lax.all_to_all(blocks, axes, split_axis=0, concat_axis=0, tiled=True)


def swap(block):
    return lax.ppermute(block, "core", [(0, 1), (1, 0)])


def contract(a, b, dims):
    return lax.dot_general(a, b, (dims, ((), ())), preferred_element_type=jnp.float32)


def per_device(
    hidden,
    queries,
    keys_values,
    out_grad,
    qkv_weight,
    out_weight,
    adapter_down_maps,
    adapter_up_maps,
):
    ring_at = lax.axis_index("z")
    core = lax.axis_index("core")
    part = ring_at.astype(jnp.int32).reshape(1)
    tokens = SEQS * PER_SEQ
    halves = LINE // SEQS
    weight_rows = MODEL_WIDTH // DEVICES

    gathered = lax.all_gather(
        jnp.concatenate([qkv_weight[0], adapter_down_maps[0]], axis=1),
        SEQ_AXES,
        axis=0,
        tiled=True,
    )
    weight_all = gathered[:, : Q_COLS + 2 * KEY_VALUE_HEADS * HEAD_SIZE]
    down_all = gathered[:, Q_COLS + 2 * KEY_VALUE_HEADS * HEAD_SIZE :]

    grad_part = jnp.broadcast_to(
        out_grad[0][:, None], (SEQS, halves, PER_SEQ, MODEL_WIDTH)
    )
    query_part = (
        queries[0].reshape(SEQS, PER_SEQ, halves, PAIR_WIDTH).transpose(0, 2, 1, 3)
    )
    row_send = jnp.concatenate([grad_part, query_part], axis=3).reshape(
        LINE, PER_SEQ, MODEL_WIDTH + PAIR_WIDTH
    )
    row_own = exchange(row_send, ("y",))
    row_other = swap(row_own)
    first = jnp.where(core == 0, row_own, row_other)
    second = jnp.where(core == 0, row_other, row_own)
    rows = jnp.stack([first, second], axis=1).reshape(
        LINE * CHUNK, MODEL_WIDTH + PAIR_WIDTH
    )
    grad_rows = rows[:, :MODEL_WIDTH]
    query_pair = rows[:, MODEL_WIDTH:]
    query_rows = jnp.where(
        core == 0, query_pair[:, :GROUP_WIDTH], query_pair[:, GROUP_WIDTH:]
    ).reshape(LINE, CHUNK, GROUP_WIDTH)

    kv_part = keys_values[0].reshape(SEQS, PER_SEQ, halves, CORES, KV_COLS).transpose(0, 2, 3, 1, 4)
    kv_send = jnp.broadcast_to(
        kv_part[:, :, None], (SEQS, halves, RING, CORES, PER_SEQ, KV_COLS)
    ).reshape(DEVICES, PER_SEQ, KV_COLS)
    kv = exchange(kv_send, SEQ_AXES).reshape(TILES, TILE, KV_COLS)
    turned = kv.transpose(0, 2, 1)
    out_part = (
        out_weight[0].reshape(weight_rows, halves, CORES, GROUP_WIDTH).transpose(1, 2, 0, 3)
    )
    out_send = jnp.broadcast_to(
        out_part[None, :, None], (SEQS, halves, RING, CORES, weight_rows, GROUP_WIDTH)
    ).reshape(DEVICES, weight_rows, GROUP_WIDTH)
    out_all = exchange(out_send, SEQ_AXES).reshape(MODEL_WIDTH, GROUP_WIDTH)

    attn_out, log_total = attend_forward(part, query_rows, kv, turned)
    attn_grad = dot(grad_rows, out_all).astype(jnp.bfloat16).reshape(LINE, CHUNK, GROUP_WIDTH)
    query_gradient, kv_grad = attend_backward(
        part, query_rows, attn_grad, kv, turned, attn_out, log_total
    )

    query_back = exchange(
        query_gradient.reshape(LINE * CORES, PER_SEQ, GROUP_WIDTH), ("y", "core")
    )
    kv_back = exchange(kv_grad.reshape(DEVICES, PER_SEQ, KV_COLS), SEQ_AXES)
    query_local = (
        query_back.reshape(SEQS, halves * CORES, PER_SEQ, GROUP_WIDTH)
        .transpose(0, 2, 1, 3)
        .reshape(tokens, Q_COLS)
    )
    kv_local = (
        jnp.sum(
            kv_back.reshape(SEQS, halves, RING, CORES, PER_SEQ, KV_COLS).astype(jnp.float32), axis=2
        )
        .astype(jnp.bfloat16)
        .reshape(SEQS, KEY_VALUE_HEADS, PER_SEQ, 2, HEAD_SIZE)
        .transpose(0, 2, 3, 1, 4)
        .reshape(tokens, 2 * KEY_VALUE_HEADS * HEAD_SIZE)
    )
    grad_qkv = jnp.concatenate([query_local, kv_local], axis=1)
    value_local = kv_local[:, KEY_VALUE_HEADS * HEAD_SIZE :]
    up_maps = adapter_up_maps[0]
    adapter_between = jnp.concatenate(
        [
            contract(query_local, up_maps[:, :Q_COLS], ((1,), (1,))),
            contract(value_local, up_maps[:, Q_COLS:], ((1,), (1,))),
        ],
        axis=1,
    ).astype(jnp.bfloat16)
    adapter_scale = ADAPTER_NUMER / ADAPTER_RANK
    input_gradient = contract(grad_qkv, weight_all, ((1,), (1,)))
    input_gradient = input_gradient + adapter_scale * contract(
        adapter_between, down_all, ((1,), (1,))
    )
    input_gradient = input_gradient.astype(jnp.bfloat16).reshape(1, SEQS, PER_SEQ, MODEL_WIDTH)
    sections = lax.axis_size("section")
    passed = lax.ppermute(
        input_gradient, "section", [((i + 1) % sections, i) for i in range(sections)]
    )

    hidden_rows = hidden[0].reshape(tokens, MODEL_WIDTH)
    adapter_reduced = dot(hidden_rows, down_all).astype(jnp.bfloat16)
    a_term = contract(hidden_rows, adapter_between, ((0,), (0,)))
    b_term = jnp.concatenate(
        [
            contract(adapter_reduced[:, :ADAPTER_RANK], query_local, ((0,), (0,))),
            contract(adapter_reduced[:, ADAPTER_RANK:], value_local, ((0,), (0,))),
        ],
        axis=1,
    )
    b_cols = b_term.shape[1] // DEVICES
    a_send = a_term.astype(jnp.bfloat16).reshape(DEVICES, weight_rows * 2 * ADAPTER_RANK)
    b_send = (
        b_term.astype(jnp.bfloat16)
        .reshape(ADAPTER_RANK, DEVICES, b_cols)
        .transpose(1, 0, 2)
        .reshape(DEVICES, ADAPTER_RANK * b_cols)
    )
    terms = exchange(jnp.concatenate([a_send, b_send], axis=1), SEQ_AXES)
    sums = (adapter_scale / GRADIENT_SCALE) * jnp.sum(terms.astype(jnp.float32), axis=0)
    a_sum = sums[: a_send.shape[1]].reshape(1, weight_rows, 2 * ADAPTER_RANK)
    b_sum = sums[a_send.shape[1] :].reshape(1, ADAPTER_RANK, b_cols)
    return (passed, a_sum, b_sum)


def solution(mesh):
    sections = mesh.shape["section"]
    fine = Mesh(mesh.devices.reshape(sections, LINE, RING, CORES), ("section",) + SEQ_AXES)
    return jax.shard_map(
        per_device,
        mesh=fine,
        in_specs=(
            P("section", None, SEQ_AXES, None),
            P("section", None, SEQ_AXES, None),
            P("section", None, SEQ_AXES, None),
            P("section", None, SEQ_AXES, None),
            P("section", SEQ_AXES, None),
            P("section", SEQ_AXES, None),
            P("section", SEQ_AXES, None),
            P("section", None, None),
        ),
        out_specs=(
            P("section", None, SEQ_AXES, None),
            P("section", SEQ_AXES, None),
            P("section", None, SEQ_AXES),
        ),
        check_vma=False,
    )
```

time: 1320 us -> 278 us (0.21)
  waiting for transfers between devices: 894 us -> 140 us
  matrix products: 126 us -> 11.2 us
  blocking collectives: 121 us -> 14.8 us
  local copies, waits for them, and re-layouts: 65.7 us -> 14.5 us
  loops' own time: 27.8 us -> 0 us
  Pallas kernels: 0 us -> 27.2 us
    unnamed x6 -> x1, waiting for transfers between devices: 762 us -> 0.02 us
    all_gather x1 -> x0, blocking collectives: 121 us -> none  [per_device(): lax.all_gather(adapter_down_maps[0], 'seq', axis=0, tiled=True)]
    dot_general x79 -> x9, matrix products: 126 us -> 11.2 us  [the longest x7 7.24 us: contract(): lax.dot_general(a, b, (dims, ((), ())), preferred_element_type=jnp.float32)]
    all_gather x2 -> x1, waiting for transfers between devices: 107 us -> 0.02 us  [per_device(): lax.all_gather(jnp.concatenate([qkv_weight[0], adapter_down_maps[0]], axi...]
    all_to_all x5, waiting for transfers between devices: 24.8 us -> 122 us  [exchange(): return lax.all_to_all(blocks, axes, split_axis=0, concat_axis=0, tiled=True)]
    dynamic_slice x140 -> x0, local copies, waits for them, and re-layouts: 36.1 us -> none  [the longest x40 23.5 us: attend(): lax.scan(row_stats, start_state, (tile_first, tile_second))]
    another operation x2 -> x0, loops' own time: 27.8 us -> none  [the longest x1 14.1 us: attend(): lax.scan(tile_grads, grad_state, (tile_first, tile_second))]
    pallas_call x0 -> x2, Pallas kernels: none -> 27.2 us  [the longest x1 15.7 us: attend_backward(): pl.pallas_call(backward_kernel, out_shape=(jax.ShapeDtypeStruct((LINE, CH...]
  transfers between devices with their start and end apart: 10 -> 8, of which waited for: 6 -> 6; matrix products, arithmetic and copies ran while one was open for 16% -> 7% of each run, Pallas kernels for 0% -> 10%
where the time goes in v1:
time: 278 us; the launch traced here: 276 us
  waiting for transfers between devices  140 us (50%)
  starting transfers between devices  45.9 us (17%)
  Pallas kernels  27.2 us (10%)
  blocking collectives  14.8 us (5%)
  local copies, waits for them, and re-layouts  14.5 us (5%)
  between operations  14.4 us (5%)
  matrix products  11.2 us (4%)
  other arithmetic  7.7 us (3%)
    all_to_all x5, waiting for transfers between devices, exchange(): return lax.all_to_all(blocks, axes, split_axis=0, concat_axis=0, tiled=True)  122 us
    all_to_all x5, starting transfers between devices, exchange(): return lax.all_to_all(blocks, axes, split_axis=0, concat_axis=0, tiled=True)  36.5 us
    ppermute x1, waiting for transfers between devices, per_device(): lax.ppermute(input_gradient, 'section', [((i + 1) % sections, i) for i in...  18.8 us
    pallas_call x1, Pallas kernels, attend_backward(): pl.pallas_call(backward_kernel, out_shape=(jax.ShapeDtypeStruct((LINE, CH...  15.7 us
    all_to_all x1, blocking collectives, exchange(): return lax.all_to_all(blocks, axes, split_axis=0, concat_axis=0, tiled=True)  14.8 us
    pallas_call x1, Pallas kernels, attend_forward(): pl.pallas_call(forward_kernel, out_shape=(jax.ShapeDtypeStruct((LINE, HEA...  11.4 us
    ppermute x1, starting transfers between devices, per_device(): lax.ppermute(input_gradient, 'section', [((i + 1) % sections, i) for i in...  7.4 us
    dot_general x7, matrix products, contract(): lax.dot_general(a, b, (dims, ((), ())), preferred_element_type=jnp.float32)  7.24 us
  transfers between devices with their start and end apart: 8, of which 6 were waited for; matrix products, arithmetic and copies ran while one was open for 7% of the time, Pallas kernels for 10%

profile of v1, /device:TPU:6, one launch (start us, length us, event | category | flops | bytes accessed | tf_op | source)
XLA Modules:
  0.0 276.0 jit_solution(4120086928679630282)
XLA Ops:
  7.2 1.6 pad_maximum_fusion.3
  8.9 1.2 reshape_squeeze.12
  10.1 1.2 broadcast_in_dim.9
  11.2 1.2 pad_maximum_fusion.1
  12.5 4.9 %all-to-all-start = ((bf16[4,64,2560]{2,1,0:T(8,128)(2,1)}), bf16[4,64,2560]{2,1,0:T(8,128)(2,1)}, u32[]{:S(2)}, u32[]{:S(2)}) async-start(bf16[4,64,2560]{2,1,0:T(8,128)(2,1)} %bitcast.3), calls=%async_computation | async-start | bytes 2621440 | tf_op jit(solution)/shard_map/all_to_all | solution.py:175
  17.4 36.1 %all-to-all-done = bf16[4,64,2560]{2,1,0:T(8,128)(2,1)} async-done(((bf16[4,64,2560]{2,1,0:T(8,128)(2,1)}), bf16[4,64,2560]{2,1,0:T(8,128)(2,1)}, u32[]{:S(2)}, u32[]{:S(2)}) %all-to-all-start) | async-done | bytes 1310752 | tf_op jit(solution)/shard_map/all_to_all | solution.py:175
  53.6 1.2 broadcast_in_dim.22
  54.8 13.3 %all-to-all-start.2 = ((bf16[64,64,128]{2,1,0:T(8,128)(2,1)}), bf16[64,64,128]{2,1,0:T(8,128)(2,1)S(1)}, u32[]{:S(2)}, u32[]{:S(2)}) async-start(bf16[64,64,128]{2,1,0:T(8,128)(2,1)} %bitcast.14), calls=%async_computation.2 | async-start | bytes 2097152 | tf_op jit(solution)/shard_map/all_to_all | solution.py:175
  68.1 2.0 collective-permute-start
  70.2 30.2 %all-to-all-done.2 = bf16[64,64,128]{2,1,0:T(8,128)(2,1)S(1)} async-done(((bf16[64,64,128]{2,1,0:T(8,128)(2,1)}), bf16[64,64,128]{2,1,0:T(8,128)(2,1)S(1)}, u32[]{:S(2)}, u32[]{:S(2)}) %all-to-all-start.2) | async-done | bytes 1048608 | tf_op jit(solution)/shard_map/all_to_all | solution.py:175
  100.4 1.1 broadcast_in_dim.10
  101.5 6.5 %all-to-all-start.1 = ((bf16[64,32,256]{2,1,0:T(8,128)(2,1)}), bf16[64,32,256]{2,1,0:T(8,128)(2,1)}, u32[]{:S(2)}, u32[]{:S(2)}) async-start(bf16[64,32,256]{2,1,0:T(8,128)(2,1)} %bitcast.10), calls=%async_computation.1 | async-start | bytes 2097152 | tf_op jit(solution)/shard_map/all_to_all | solution.py:175
  108.6 1.9 select_bitcast_fusion.1
  110.8 1.5 copy-done.2
  112.3 11.4 %attention_forward.1 = (f32[4,64,512]{2,1,0:T(8,128)S(1)}, f32[4,1,512]{2,1,0:T(1,128)S(1)}) custom-call(s32[1]{0:T(128)} %bitcast.part_ref, bf16[4,128,256]{2,1,0:T(8,128)(2,1)S(1)} %bitcast.66, bf16[4,1024,128]{2,1,0:T(8,128)(2,1)S(1)} %bitcast.62, bf16[4,128,1024]{2,1,0:T(8,128)(2,1)S(1)} %bitcast.64), custom_call_target="tpu_custom_call" | custom-call | tf_op jit(solution)/shard_map/attention_forward/pallas_call | solution.py:146
  123.7 16.4 %all-to-all-done.1 = bf16[64,32,256]{2,1,0:T(8,128)(2,1)} async-done(((bf16[64,32,256]{2,1,0:T(8,128)(2,1)}), bf16[64,32,256]{2,1,0:T(8,128)(2,1)}, u32[]{:S(2)}, u32[]{:S(2)}) %all-to-all-start.1) | async-done | bytes 1048608 | tf_op jit(solution)/shard_map/all_to_all | solution.py:175
  140.2 2.6 fusion.7
  142.7 15.7 %attention_backward.1 = (bf16[4,128,256]{2,1,0:T(8,128)(2,1)S(1)}, bf16[4,1024,128]{2,1,0:T(8,128)(2,1)S(1)}) custom-call(s32[1]{0:T(128)} %bitcast.part_ref, bf16[4,128,256]{2,1,0:T(8,128)(2,1)S(1)} %bitcast.67, bf16[4,128,256]{2,1,0:T(8,128)(2,1)S(1)} %bitcast.70, bf16[4,1024,128]{2,1,0:T(8,128)(2,1)S(1)} %bitcast.63, bf16[4,128,1024]{2,1,0:T(8,128)(2,1)S(1)} %bitcast.65, ...), custom_call_target="tpu_custom_call" | custom-call | tf_op jit(solution)/shard_map/attention_backward/pallas_call | solution.py:160
  158.5 1.0 copy-done.1
  159.4 14.8 %all_to_all.34 = bf16[8,64,256]{2,1,0:T(8,128)(2,1)S(1)} all-to-all(bf16[8,64,256]{2,1,0:T(8,128)(2,1)S(1)} %bitcast.69), channel_id=1, replica_groups=mesh['section'=8,'y'=4,'z'=8,'core'=2] {'y','core'}, dimensions={0} | all-to-all | bytes 524288 | tf_op jit(solution)/shard_map/all_to_all | solution.py:175
  174.3 5.4 %all-to-all-start.4 = ((bf16[64,64,128]{2,1,0:T(8,128)(2,1)}), bf16[64,64,128]{2,1,0:T(8,128)(2,1)S(1)}, u32[]{:S(2)}, u32[]{:S(2)}) async-start(bf16[64,64,128]{2,1,0:T(8,128)(2,1)} %bitcast.68), calls=%async_computation.4 | async-start | bytes 2097152 | tf_op jit(solution)/shard_map/all_to_all | solution.py:175
  180.2 28.2 %all-to-all-done.4 = bf16[64,64,128]{2,1,0:T(8,128)(2,1)S(1)} async-done(((bf16[64,64,128]{2,1,0:T(8,128)(2,1)}), bf16[64,64,128]{2,1,0:T(8,128)(2,1)S(1)}, u32[]{:S(2)}, u32[]{:S(2)}) %all-to-all-start.4) | async-done | bytes 1048608 | tf_op jit(solution)/shard_map/all_to_all | solution.py:175
  210.3 1.4 fusion.10
  213.6 1.1 reduce.2
  214.7 1.0 reshape.99
  215.7 6.3 %all-to-all-start.5 = ((bf16[64,2,2688]{2,1,0:T(2,128)(2,1)}), bf16[64,2,2688]{2,1,0:T(2,128)(2,1)S(1)}, u32[]{:S(2)}, u32[]{:S(2)}) async-start(bf16[64,2,2688]{2,1,0:T(2,128)(2,1)} %reshape.99), calls=%async_computation.5 | async-start | bytes 1376256 | tf_op jit(solution)/shard_map/all_to_all | solution.py:175
  222.1 4.9 %fusion = f32[128,2048]{1,0:T(8,128)S(1)} fusion(bf16[2048,1664]{1,0:T(8,128)(2,1)} %all-gather.2.cloned.1.call-done, bf16[128,512]{1,0:T(8,128)(2,1)S(1)} %reshape.93, bf16[128,1024]{1,0:T(8,128)(2,1)S(1)} %bitcast.76), kind=kOutput, calls=%fused_computation | convolution fusion | flops 806092800 | bytes 7733248 | tf_op jit(solution)/shard_map/dot_general | solution.py:183
  227.0 1.4 fusion.3
  228.4 7.4 %collective-permute-start.1 = (bf16[1,2,64,2048]{3,2,1,0:T(8,128)(2,1)S(1)}, bf16[1,2,64,2048]{3,2,1,0:T(8,128)(2,1)S(1)}, u32[]{:S(2)}, u32[]{:S(2)}) collective-permute-start(bf16[1,2,64,2048]{3,2,1,0:T(8,128)(2,1)S(1)} %bitcast.84), channel_id=1, source_target_pairs={{64,0},{128,64},{192,128},{256,192},{320,256},{384,320},{448,384},... | collective-permute-start | bytes 1572872 | tf_op jit(solution)/shard_map/ppermute | solution.py:289
  235.8 18.8 %collective-permute-done.1 = bf16[1,2,64,2048]{3,2,1,0:T(8,128)(2,1)S(1)} collective-permute-done((bf16[1,2,64,2048]{3,2,1,0:T(8,128)(2,1)S(1)}, bf16[1,2,64,2048]{3,2,1,0:T(8,128)(2,1)S(1)}, u32[]{:S(2)}, u32[]{:S(2)}) %collective-permute-start.1) | collective-permute-done | bytes 524320 | tf_op jit(solution)/shard_map/ppermute | solution.py:289
  254.5 10.6 %all-to-all-done.5 = bf16[64,2,2688]{2,1,0:T(2,128)(2,1)S(1)} async-done(((bf16[64,2,2688]{2,1,0:T(2,128)(2,1)}), bf16[64,2,2688]{2,1,0:T(2,128)(2,1)S(1)}, u32[]{:S(2)}, u32[]{:S(2)}) %all-to-all-start.5) | async-done | bytes 688160 | tf_op jit(solution)/shard_map/all_to_all | solution.py:175
  265.6 1.3 convert_reduce_fusion
  (50 shorter events, 7.9 us)
Async XLA Ops:
  7.2 202.3 %copy-start = (bf16[1,2,64,2048]{3,2,1,0:T(8,128)(2,1)S(1)}, bf16[1,2,64,2048]{3,2,1,0:T(8,128)(2,1)}, u32[]{:S(2)}) copy-start(bf16[1,2,64,2048]{3,2,1,0:T(8,128)(2,1)} %param.8) | copy-start | bytes 1572868
  7.2 203.1 %all-gather.2.cloned.1.call-start = ((), (), s32[]{:S(2)}) async-start(), calls=%async_computation.6 | async-start | bytes 6922240 | tf_op jit(solution)/shard_map/all_gather | solution.py:203
  11.2 6.1 %copy-start.3 = (bf16[1,2,64,512]{3,2,1,0:T(8,128)(2,1)S(1)}, bf16[1,2,64,512]{3,2,1,0:T(8,128)(2,1)}, u32[]{:S(2)}) copy-start(bf16[1,2,64,512]{3,2,1,0:T(8,128)(2,1)} %param.10) | copy-start | bytes 393220
  12.5 41.1 %all-to-all-start = ((bf16[4,64,2560]{2,1,0:T(8,128)(2,1)}), bf16[4,64,2560]{2,1,0:T(8,128)(2,1)}, u32[]{:S(2)}, u32[]{:S(2)}) async-start(bf16[4,64,2560]{2,1,0:T(8,128)(2,1)} %bitcast.3), calls=%async_computation | async-start | bytes 2621440 | tf_op jit(solution)/shard_map/all_to_all | solution.py:175
  17.3 52.8 %copy-start.5 = (bf16[1,32,1024]{2,1,0:T(8,128)(2,1)S(1)}, bf16[1,32,1024]{2,1,0:T(8,128)(2,1)}, u32[]{:S(2)}) copy-start(bf16[1,32,1024]{2,1,0:T(8,128)(2,1)} %param.13) | copy-start | bytes 196612
  54.8 45.6 %all-to-all-start.2 = ((bf16[64,64,128]{2,1,0:T(8,128)(2,1)}), bf16[64,64,128]{2,1,0:T(8,128)(2,1)S(1)}, u32[]{:S(2)}, u32[]{:S(2)}) async-start(bf16[64,64,128]{2,1,0:T(8,128)(2,1)} %bitcast.14), calls=%async_computation.2 | async-start | bytes 2097152 | tf_op jit(solution)/shard_map/all_to_all | solution.py:175
  68.1 40.4 %collective-permute-start = (bf16[4,64,2560]{2,1,0:T(8,128)(2,1)}, bf16[4,64,2560]{2,1,0:T(8,128)(2,1)}, u32[]{:S(2)}, u32[]{:S(2)}) collective-permute-start(bf16[4,64,2560]{2,1,0:T(8,128)(2,1)} %all-to-all-done), channel_id=1, source_target_pairs={{0,1},{1,0},{2,3},{3,2},{4,5},{5,4},{6,7},{7,6},{8,9},{9,8},{10,11... | collective-permute-start | bytes 3932168 | tf_op jit(solution)/shard_map/ppermute | solution.py:179
  101.5 38.6 %all-to-all-start.1 = ((bf16[64,32,256]{2,1,0:T(8,128)(2,1)}), bf16[64,32,256]{2,1,0:T(8,128)(2,1)}, u32[]{:S(2)}, u32[]{:S(2)}) async-start(bf16[64,32,256]{2,1,0:T(8,128)(2,1)} %bitcast.10), calls=%async_computation.1 | async-start | bytes 2097152 | tf_op jit(solution)/shard_map/all_to_all | solution.py:175
  110.7 1.6 copy-start.2
  158.5 1.0 copy-start.1
  159.4 20.5 %copy-start.4 = (bf16[1,64,1280]{2,1,0:T(8,128)(2,1)S(1)}, bf16[1,64,1280]{2,1,0:T(8,128)(2,1)}, u32[]{:S(2)}) copy-start(bf16[1,64,1280]{2,1,0:T(8,128)(2,1)} %param.15) | copy-start | bytes 491524
  174.3 34.1 %all-to-all-start.4 = ((bf16[64,64,128]{2,1,0:T(8,128)(2,1)}), bf16[64,64,128]{2,1,0:T(8,128)(2,1)S(1)}, u32[]{:S(2)}, u32[]{:S(2)}) async-start(bf16[64,64,128]{2,1,0:T(8,128)(2,1)} %bitcast.68), calls=%async_computation.4 | async-start | bytes 2097152 | tf_op jit(solution)/shard_map/all_to_all | solution.py:175
  215.7 49.3 %all-to-all-start.5 = ((bf16[64,2,2688]{2,1,0:T(2,128)(2,1)}), bf16[64,2,2688]{2,1,0:T(2,128)(2,1)S(1)}, u32[]{:S(2)}, u32[]{:S(2)}) async-start(bf16[64,2,2688]{2,1,0:T(2,128)(2,1)} %reshape.99), calls=%async_computation.5 | async-start | bytes 1376256 | tf_op jit(solution)/shard_map/all_to_all | solution.py:175
  228.4 26.2 %collective-permute-start.1 = (bf16[1,2,64,2048]{3,2,1,0:T(8,128)(2,1)S(1)}, bf16[1,2,64,2048]{3,2,1,0:T(8,128)(2,1)S(1)}, u32[]{:S(2)}, u32[]{:S(2)}) collective-permute-start(bf16[1,2,64,2048]{3,2,1,0:T(8,128)(2,1)S(1)} %bitcast.84), channel_id=1, source_target_pairs={{64,0},{128,64},{192,128},{256,192},{320,256},{384,320},{448,384},... | collective-permute-start | bytes 1572872 | tf_op jit(solution)/shard_map/ppermute | solution.py:289
Sparse Core Ops, SparseCore 0:
  10.7 190.6 all-gather.1

commit v2 on v1

v2 whole, which is shorter than its diff:
```python
import jax
import jax.numpy as jnp
from jax import lax
from jax.experimental import pallas as pl
from jax.experimental.pallas import tpu as pltpu
from jax.sharding import Mesh, PartitionSpec as P

MODEL_WIDTH = 2048
QUERY_HEADS = 16
KEY_VALUE_HEADS = 4
HEAD_SIZE = 64
ADAPTER_RANK = 64
ADAPTER_NUMER = 128
GRADIENT_SCALE = 32
SEQS = 2
LEN = 4096

LINE = 4
RING = 8
CORES = 2
SEQ_AXES = ("y", "z", "core")
DEVICES = LINE * RING * CORES
PER_SEQ = LEN // DEVICES
Q_COLS = QUERY_HEADS * HEAD_SIZE
KV_COLS = 2 * HEAD_SIZE
GROUP = QUERY_HEADS // KEY_VALUE_HEADS
GROUP_WIDTH = GROUP * HEAD_SIZE
PAIR_WIDTH = CORES * GROUP_WIDTH
WEIGHT_ROWS = MODEL_WIDTH // DEVICES
B_ROWS = (QUERY_HEADS + KEY_VALUE_HEADS) * HEAD_SIZE // DEVICES // 2
ADAPTER_SCALE = ADAPTER_NUMER / ADAPTER_RANK
TERM_SCALE = ADAPTER_SCALE / GRADIENT_SCALE
ROW_COLS = MODEL_WIDTH + PAIR_WIDTH
WEIGHT_COLS = Q_COLS + 2 * KEY_VALUE_HEADS * HEAD_SIZE + 2 * ADAPTER_RANK
FOLD = 896

CHUNK = CORES * PER_SEQ
SPAN = RING * CHUNK
COLS = GROUP * CHUNK
TILE = SPAN
EXP_SCALE = HEAD_SIZE ** (-0.5) * 1.4426950408889634


def dot(a, b):
    return jnp.dot(a, b, preferred_element_type=jnp.float32)


def contract(a, b, dims):
    return lax.dot_general(a, b, (dims, ((), ())), preferred_element_type=jnp.float32)


def head_columns(rows):
    turned = rows.astype(jnp.float32).T
    return jnp.concatenate(
        [turned[h * HEAD_SIZE : (h + 1) * HEAD_SIZE] for h in range(GROUP)], axis=1
    )


def causal_mask(part, core):
    key_pos = lax.broadcasted_iota(jnp.int32, (TILE, COLS), 0)
    row = lax.broadcasted_iota(jnp.int32, (TILE, COLS), 1) % CHUNK
    row_pos = part * CHUNK + (row + core * PER_SEQ) % CHUNK
    return row_pos >= key_pos


def tile_of(pair_ref, t):
    return pair_ref[:, t, :, :PER_SEQ, :].reshape(TILE, KV_COLS)


def query_rows_of(own_ref, other_ref, j, core):
    columns = pl.ds(pl.multiple_of(MODEL_WIDTH + core * GROUP_WIDTH, GROUP_WIDTH), GROUP_WIDTH)
    return jnp.concatenate([own_ref[j, :, columns], other_ref[j, :, columns]], axis=0)


def attention_kernel(
    place_ref, own_ref, other_ref, pair_ref, dq_ref, dkv_ref, acc_ref, turned_ref, weight_ref
):
    part, core = place_ref[0], place_ref[1]
    scale = HEAD_SIZE ** (-0.5)
    acc_ref[...] = jnp.zeros_like(acc_ref)

    def prepare(t, carry):
        turned_ref[t] = tile_of(pair_ref, t).T
        for z in range(RING):
            for c in range(CORES):
                block = pair_ref[z, t, c, PER_SEQ:, :]
                weight_ref[t, z, c] = jnp.concatenate(
                    [block[:WEIGHT_ROWS], block[WEIGHT_ROWS:]], axis=1
                )
        return carry

    lax.fori_loop(0, LINE, prepare, 0)
    weight = weight_ref[...].reshape(MODEL_WIDTH, GROUP_WIDTH)

    def chunk(j, carry):
        query_half = head_columns(query_rows_of(own_ref, other_ref, j, core))
        out_grad = jnp.concatenate(
            [own_ref[j, :, :MODEL_WIDTH], other_ref[j, :, :MODEL_WIDTH]], axis=0
        )
        grad_half = head_columns(dot(out_grad, weight).astype(jnp.bfloat16))
        blank = jnp.zeros_like(query_half)
        query_full = jnp.concatenate([query_half, blank], axis=0)
        grad_full = jnp.concatenate([blank, grad_half], axis=0)
        query_cols = query_full.astype(jnp.bfloat16)
        grad_cols = grad_full.astype(jnp.bfloat16)
        query_rows = query_full.T.astype(jnp.bfloat16)
        grad_rows = grad_full.T.astype(jnp.bfloat16)

        def scores_of(t, masked):
            scores = dot(tile_of(pair_ref, t), query_cols)
            if masked:
                scores = jnp.where(causal_mask(part, core), scores, -jnp.inf)
            return scores

        def forward_tile(t, state, masked):
            top, total, mixed = state
            scores = scores_of(t, masked)
            new_top = jnp.maximum(top, jnp.max(scores, axis=0, keepdims=True))
            shrink = jnp.exp2((top - new_top) * EXP_SCALE)
            power = jnp.exp2(scores * EXP_SCALE - new_top * EXP_SCALE)
            total = total * shrink + jnp.sum(power, axis=0, keepdims=True)
            mixed = mixed * shrink + dot(turned_ref[t, HEAD_SIZE:], power.astype(jnp.bfloat16))
            return new_top, total, mixed

        state = (
            jnp.full((1, COLS), -jnp.inf, jnp.float32),
            jnp.zeros((1, COLS), jnp.float32),
            jnp.zeros((HEAD_SIZE, COLS), jnp.float32),
        )
        state = lax.fori_loop(0, j, lambda t, s: forward_tile(t, s, False), state)
        top, total, mixed = forward_tile(j, state, True)
        delta = jnp.sum(grad_half * (mixed / total), axis=0, keepdims=True)
        log_total = top * EXP_SCALE + jnp.log2(total)

        def backward_tile(t, query_sum, masked):
            prob = jnp.exp2(scores_of(t, masked) * EXP_SCALE - log_total)
            prob_grad = dot(tile_of(pair_ref, t), grad_cols)
            score_grad = (prob * (prob_grad - delta)).astype(jnp.bfloat16)
            acc_ref[t] += dot(score_grad, query_rows) + dot(prob.astype(jnp.bfloat16), grad_rows)
            return query_sum + dot(turned_ref[t, :HEAD_SIZE], score_grad)

        query_sum = lax.fori_loop(
            0,
            j,
            lambda t, s: backward_tile(t, s, False),
            jnp.zeros((HEAD_SIZE, COLS), jnp.float32),
        )
        query_sum = backward_tile(j, query_sum, True) * scale
        stacked = jnp.concatenate(
            [query_sum[:, h * CHUNK : (h + 1) * CHUNK] for h in range(GROUP)], axis=0
        )
        dq_ref[j] = stacked.T.astype(jnp.bfloat16).reshape(CORES, PER_SEQ, GROUP_WIDTH)
        return carry

    lax.fori_loop(0, LINE, chunk, 0)
    lane = lax.broadcasted_iota(jnp.int32, (TILE, KV_COLS), 1)
    factor = jnp.where(lane < HEAD_SIZE, scale, 1.0)

    def finish(t, carry):
        dkv_ref[t] = (
            (acc_ref[t] * factor).astype(jnp.bfloat16).reshape(RING * CORES, PER_SEQ, KV_COLS)
        )
        return carry

    lax.fori_loop(0, LINE, finish, 0)


def input_kernel(place_ref, query_ref, rest_ref, own_ref, other_ref, out_ref):
    core = place_ref[1]
    query, rest = query_ref[...], rest_ref[...]
    part = RING // 2
    for y in range(LINE):
        for half in range(2):
            ring = slice(half * part, (half + 1) * part)
            own, other = own_ref[ring, y], other_ref[ring, y]
            weight = jnp.stack(
                [jnp.where(core == 0, own, other), jnp.where(core == 0, other, own)], axis=1
            ).reshape(part * CORES * WEIGHT_ROWS, -1)
            product = contract(query, weight[:, :Q_COLS], ((1,), (1,))) + contract(
                rest, weight[:, Q_COLS : Q_COLS + rest.shape[1]], ((1,), (1,))
            )
            width = product.shape[1]
            at = (2 * y + half) * width
            out_ref[:, at : at + width] = product.astype(jnp.bfloat16)


def term_kernel(terms_ref, a_ref, b_ref, held_ref):
    total = jnp.sum(terms_ref[...].astype(jnp.float32), axis=0) * TERM_SCALE
    a_ref[...] = total[:WEIGHT_ROWS]
    held_ref[...] = jnp.zeros_like(held_ref)
    held_ref[:B_ROWS] = total[WEIGHT_ROWS:]
    turned = held_ref[...].T
    b_ref[:, :B_ROWS] = turned[:ADAPTER_RANK, :B_ROWS]
    b_ref[:, B_ROWS:] = turned[ADAPTER_RANK:, :B_ROWS]


VMEM = pl.BlockSpec(memory_space=pltpu.VMEM)
SMEM = pl.BlockSpec(memory_space=pltpu.SMEM)
PARAMS = pltpu.CompilerParams(vmem_limit_bytes=48 * 2**20)


def attend(place, own, other, pairs):
    return pl.pallas_call(
        attention_kernel,
        out_shape=(
            jax.ShapeDtypeStruct((LINE, CORES, PER_SEQ, GROUP_WIDTH), jnp.bfloat16),
            jax.ShapeDtypeStruct((LINE, RING * CORES, PER_SEQ, KV_COLS), jnp.bfloat16),
        ),
        in_specs=[SMEM] + [VMEM] * 3,
        out_specs=(VMEM, VMEM),
        scratch_shapes=[
            pltpu.VMEM((LINE, TILE, KV_COLS), jnp.float32),
            pltpu.VMEM((LINE, KV_COLS, TILE), jnp.bfloat16),
            pltpu.VMEM((LINE, RING, CORES, WEIGHT_ROWS, GROUP_WIDTH), jnp.bfloat16),
        ],
        compiler_params=PARAMS,
        name="attention",
    )(place, own, other, pairs)


def term_sums(terms):
    return pl.pallas_call(
        term_kernel,
        out_shape=(
            jax.ShapeDtypeStruct((WEIGHT_ROWS, 2 * ADAPTER_RANK), jnp.float32),
            jax.ShapeDtypeStruct((ADAPTER_RANK, 2 * B_ROWS), jnp.float32),
        ),
        in_specs=[VMEM],
        out_specs=(VMEM, VMEM),
        scratch_shapes=[pltpu.VMEM((2 * ADAPTER_RANK, 2 * ADAPTER_RANK), jnp.float32)],
        compiler_params=PARAMS,
        name="term_sums",
    )(terms)


def input_product(place, query, rest, own, other):
    return pl.pallas_call(
        input_kernel,
        out_shape=jax.ShapeDtypeStruct((query.shape[0], MODEL_WIDTH), jnp.bfloat16),
        in_specs=[SMEM] + [VMEM] * 4,
        out_specs=VMEM,
        compiler_params=PARAMS,
        name="input_gradient",
    )(place, query, rest, own, other)


def exchange(blocks, axes):
    return lax.all_to_all(blocks, axes, split_axis=0, concat_axis=0, tiled=True)


def swap(block):
    return lax.ppermute(block, "core", [(0, 1), (1, 0)])


def from_next(block):
    sections = lax.axis_size("section")
    return lax.ppermute(block, "section", [((i + 1) % sections, i) for i in range(sections)])


def along(block, distance):
    return lax.ppermute(block, "y", [(y, (y + distance) % LINE) for y in range(LINE)])


def by_source(pieces, line_at):
    doubled = jnp.stack(pieces[::-1] + pieces[:0:-1])
    return lax.dynamic_slice_in_dim(doubled, LINE - 1 - line_at, LINE, 0)


def core_order(own, other, core, axis):
    return jnp.stack(
        [jnp.where(core == 0, own, other), jnp.where(core == 0, other, own)], axis=axis
    )


def ordered(first, second):
    return lax.optimization_barrier((first, second))


def per_device(
    hidden,
    queries,
    keys_values,
    out_grad,
    qkv_weight,
    out_weight,
    adapter_down_maps,
    adapter_up_maps,
):
    line_at = lax.axis_index("y")
    core = lax.axis_index("core")
    place = jnp.stack([lax.axis_index("z"), core]).astype(jnp.int32)
    tokens = SEQS * PER_SEQ
    halves = LINE // SEQS
    qkv_cols = WEIGHT_COLS - 2 * ADAPTER_RANK

    kv_part = keys_values[0].reshape(SEQS, PER_SEQ, halves, CORES, KV_COLS).transpose(0, 2, 3, 1, 4)
    out_part = (
        out_weight[0]
        .reshape(WEIGHT_ROWS, halves, CORES, 2, GROUP_WIDTH // 2)
        .transpose(1, 2, 3, 0, 4)
        .reshape(1, halves, CORES, 2 * WEIGHT_ROWS, GROUP_WIDTH // 2)
    )
    group_send = jnp.concatenate(
        [kv_part, jnp.broadcast_to(out_part, (SEQS,) + out_part.shape[1:])], axis=3
    ).reshape(LINE * CORES, PER_SEQ + 2 * WEIGHT_ROWS, KV_COLS)
    group_line = exchange(group_send, ("y", "core"))

    grad_part = jnp.broadcast_to(out_grad[0][:, None], (SEQS, halves, PER_SEQ, MODEL_WIDTH))
    query_part = queries[0].reshape(SEQS, PER_SEQ, halves, PAIR_WIDTH).transpose(0, 2, 1, 3)
    weights = jnp.concatenate([qkv_weight[0], adapter_down_maps[0]], axis=1)
    folded = jnp.concatenate([weights[:, :FOLD], weights[:, WEIGHT_COLS - FOLD :]], axis=0)
    weight_part = jnp.broadcast_to(folded, (SEQS, halves, PER_SEQ, FOLD))
    row_send = jnp.concatenate([grad_part, query_part, weight_part], axis=3).reshape(
        LINE, PER_SEQ, ROW_COLS + FOLD
    )
    group_line, row_send = ordered(group_line, row_send)
    group_all = lax.all_gather(group_line, "z", axis=0).reshape(
        RING, LINE, CORES, PER_SEQ + 2 * WEIGHT_ROWS, KV_COLS
    )
    row_own = exchange(row_send, ("y",))
    row_other = swap(row_own)
    weight_line = jnp.concatenate(
        [
            row_own[:, :WEIGHT_ROWS, ROW_COLS:],
            row_own[:, WEIGHT_ROWS:, ROW_COLS + 2 * FOLD - WEIGHT_COLS :],
        ],
        axis=2,
    )
    group_all, weight_line = ordered(group_all, weight_line)
    weight_own = lax.all_gather(weight_line, "z", axis=0)

    query_gradient, kv_grad = attend(place, row_own, row_other, group_all)
    kv_back = exchange(kv_grad.reshape(DEVICES, PER_SEQ, KV_COLS), SEQ_AXES)

    query_chip = core_order(query_gradient[:, 0], swap(query_gradient[:, 1]), core, 1)
    query_sends = [
        lax.dynamic_index_in_dim(query_chip, (line_at + d) % LINE, 0, keepdims=False)
        for d in range(LINE)
    ]
    query_sends[0], weight_own = ordered(query_sends[0], weight_own)
    weight_other = swap(weight_own)
    query_back = by_source(
        query_sends[:1] + [along(query_sends[d], d) for d in range(1, LINE)], line_at
    )
    query_local = (
        query_back.reshape(SEQS, halves * CORES, PER_SEQ, GROUP_WIDTH)
        .transpose(0, 2, 1, 3)
        .reshape(tokens, Q_COLS)
    )
    kv_local = (
        jnp.sum(
            kv_back.reshape(SEQS, halves, RING, CORES, PER_SEQ, KV_COLS).astype(jnp.float32), axis=2
        )
        .astype(jnp.bfloat16)
        .reshape(SEQS, KEY_VALUE_HEADS, PER_SEQ, 2, HEAD_SIZE)
        .transpose(0, 2, 3, 1, 4)
        .reshape(tokens, 2 * KEY_VALUE_HEADS * HEAD_SIZE)
    )
    value_local = kv_local[:, KEY_VALUE_HEADS * HEAD_SIZE :]
    up_maps = adapter_up_maps[0]
    adapter_between = jnp.concatenate(
        [
            contract(query_local, up_maps[:, :Q_COLS], ((1,), (1,))),
            contract(value_local, up_maps[:, Q_COLS:], ((1,), (1,))),
        ],
        axis=1,
    ).astype(jnp.bfloat16)
    down_own, down_other = weight_own[..., qkv_cols:], weight_other[..., qkv_cols:]
    down_all = (
        core_order(down_own, down_other, core, 2)
        .transpose(1, 0, 2, 3, 4)
        .reshape(MODEL_WIDTH, 2 * ADAPTER_RANK)
    )

    hidden_rows = hidden[0].reshape(tokens, MODEL_WIDTH)
    adapter_reduced = dot(hidden_rows, down_all).astype(jnp.bfloat16)
    a_term = contract(hidden_rows, adapter_between, ((0,), (0,)))
    b_turned = jnp.concatenate(
        [
            contract(query_local, adapter_reduced[:, :ADAPTER_RANK], ((0,), (0,))),
            contract(value_local, adapter_reduced[:, ADAPTER_RANK:], ((0,), (0,))),
        ],
        axis=0,
    )
    ranks = 2 * ADAPTER_RANK
    a_send = a_term.reshape(LINE * RING, CORES, WEIGHT_ROWS, ranks)
    b_send = b_turned.reshape(LINE * RING, CORES, 2, B_ROWS, ADAPTER_RANK)
    b_send = jnp.concatenate([b_send[:, :, 0], b_send[:, :, 1]], axis=3)
    term_send = jnp.concatenate([a_send, b_send], axis=2)
    kept = lax.dynamic_index_in_dim(term_send, core, 1, keepdims=False)
    given = lax.dynamic_index_in_dim(term_send, 1 - core, 1, keepdims=False)
    term_chip = (kept + swap(given)).astype(jnp.bfloat16)
    a_sum, b_sum = term_sums(exchange(term_chip, ("y", "z")))

    rest = jnp.concatenate([kv_local, adapter_between * jnp.bfloat16(ADAPTER_SCALE)], axis=1)
    input_gradient = input_product(place, query_local, rest, weight_own, weight_other)
    passed = from_next(input_gradient.reshape(1, SEQS, PER_SEQ, MODEL_WIDTH))
    return (passed, a_sum[None], b_sum[None])


def solution(mesh):
    sections = mesh.shape["section"]
    fine = Mesh(mesh.devices.reshape(sections, LINE, RING, CORES), ("section",) + SEQ_AXES)
    return jax.shard_map(
        per_device,
        mesh=fine,
        in_specs=(
            P("section", None, SEQ_AXES, None),
            P("section", None, SEQ_AXES, None),
            P("section", None, SEQ_AXES, None),
            P("section", None, SEQ_AXES, None),
            P("section", SEQ_AXES, None),
            P("section", SEQ_AXES, None),
            P("section", SEQ_AXES, None),
            P("section", None, None),
        ),
        out_specs=(
            P("section", None, SEQ_AXES, None),
            P("section", SEQ_AXES, None),
            P("section", None, SEQ_AXES),
        ),
        check_vma=False,
    )
```

time: 278 us -> 225 us (0.81)
  the two profiles are of different devices: /device:TPU:6 before, /device:TPU:62 now
where the time goes in v2:
time: 225 us; the launch traced here: 224 us
  waiting for transfers between devices  58.9 us (26%)
  starting transfers between devices  49.9 us (22%)
  blocking collectives  44.9 us (20%)
  Pallas kernels  36.9 us (16%)
  between operations  14.7 us (7%)
  local copies, waits for them, and re-layouts  11.6 us (5%)
  other arithmetic  5.94 us (3%)
    all_to_all x1, blocking collectives, exchange(): return lax.all_to_all(blocks, axes, split_axis=0, concat_axis=0, tiled=True)  44.9 us
    pallas_call x1, Pallas kernels, attend(): pl.pallas_call(attention_kernel, out_shape=(jax.ShapeDtypeStruct((LINE, C...  31.8 us
    ppermute x1, waiting for transfers between devices, from_next(): lax.ppermute(block, 'section', [((i + 1) % sections, i) for i in range(se...  28.8 us
    all_to_all x3, starting transfers between devices, exchange(): return lax.all_to_all(blocks, axes, split_axis=0, concat_axis=0, tiled=True)  28.6 us
    ppermute x3, waiting for transfers between devices, along(): lax.ppermute(block, 'y', [(y, (y + distance) % LINE) for y in range(LINE)])  14.7 us
    ppermute x3, starting transfers between devices, along(): lax.ppermute(block, 'y', [(y, (y + distance) % LINE) for y in range(LINE)])  10.9 us
    ppermute x4, starting transfers between devices, swap(): return lax.ppermute(block, 'core', [(0, 1), (1, 0)])  7.77 us
    all_to_all x3, waiting for transfers between devices, exchange(): return lax.all_to_all(blocks, axes, split_axis=0, concat_axis=0, tiled=True)  6.28 us
  transfers between devices with their start and end apart: 13, of which 9 were waited for; matrix products, arithmetic and copies ran while one was open for 2% of the time, Pallas kernels for 16%

profile of v2, /device:TPU:62, one launch (start us, length us, event | category | flops | bytes accessed | tf_op | source)
XLA Modules:
  0.0 224.1 jit_solution(1911622731859577400)
XLA Ops:
  7.2 0.9 reshape_squeeze.13
  8.2 0.9 reshape_squeeze.12
  9.9 6.3 %all-to-all-start = ((bf16[8,128,128]{2,1,0:T(8,128)(2,1)}), bf16[8,128,128]{2,1,0:T(8,128)(2,1)S(1)}, u32[]{:S(2)}, u32[]{:S(2)}) async-start(bf16[8,128,128]{2,1,0:T(8,128)(2,1)} %bitcast.5), calls=%async_computation | async-start | bytes 524288 | tf_op jit(solution)/shard_map/all_to_all | solution.py:248
  16.6 1.4 pad_maximum_fusion
  18.0 5.3 %all-to-all-done = bf16[8,128,128]{2,1,0:T(8,128)(2,1)S(1)} async-done(((bf16[8,128,128]{2,1,0:T(8,128)(2,1)}), bf16[8,128,128]{2,1,0:T(8,128)(2,1)S(1)}, u32[]{:S(2)}, u32[]{:S(2)}) %all-to-all-start) | async-done | bytes 262176 | tf_op jit(solution)/shard_map/all_to_all | solution.py:248
  24.1 44.9 %all_to_all.20.own_ref = bf16[4,64,3456]{2,1,0:T(8,128)(2,1)S(1)} all-to-all(bf16[4,64,3456]{2,1,0:T(8,128)(2,1)} %bitcast.110), channel_id=1, replica_groups=mesh['section'=8,'y'=4,'z'=8,'core'=2] {'y'}, dimensions={0} | all-to-all | bytes 3538944 | tf_op jit(solution)/shard_map/all_to_all | solution.py:248
  69.8 2.7 %all-gather.5.cloned.1.call-done = bf16[64,128,128]{2,1,0:T(8,128)(2,1)} async-done(((bf16[8,128,128]{2,1,0:T(8,128)(2,1)}), bf16[64,128,128]{2,1,0:T(8,128)(2,1)}) %all-gather.5.cloned.1.call-update) | async-done | bytes 2097168 | tf_op jit(solution)/shard_map/all_gather | solution.py:317
  72.5 1.9 collective-permute-start
  74.5 3.7 %collective-permute-done.other_ref = bf16[4,64,3456]{2,1,0:T(8,128)(2,1)} collective-permute-done((bf16[4,64,3456]{2,1,0:T(8,128)(2,1)S(1)}, bf16[4,64,3456]{2,1,0:T(8,128)(2,1)}, u32[]{:S(2)}, u32[]{:S(2)}) %collective-permute-start) | collective-permute-done | bytes 1769504 | tf_op jit(solution)/shard_map/ppermute | solution.py:252
  78.2 31.8 %attention.1 = (bf16[4,2,64,256]{3,2,1,0:T(8,128)(2,1)S(1)}, bf16[4,16,64,128]{3,2,1,0:T(8,128)(2,1)}) custom-call(s32[2]{0:T(128)S(1)} %pad_add_fusion.place_ref, bf16[4,64,3456]{2,1,0:T(8,128)(2,1)S(1)} %all_to_all.20.own_ref, bf16[4,64,3456]{2,1,0:T(8,128)(2,1)} %collective-permute-done.other_ref, bf16[8,4,2,128,128]{4,3,2,1,0:T(8,128)(2,1)} %bitcast.113), custom_call_target="tpu_custom_call" | custom-call | tf_op jit(solution)/shard_map/attention/pallas_call | solution.py:203
  110.1 2.0 collective-permute-start.1
  112.1 11.7 %all-to-all-start.2 = ((bf16[64,64,128]{2,1,0:T(8,128)(2,1)}), bf16[64,64,128]{2,1,0:T(8,128)(2,1)S(1)}, u32[]{:S(2)}, u32[]{:S(2)}) async-start(bf16[64,64,128]{2,1,0:T(8,128)(2,1)} %bitcast.27), calls=%async_computation.2 | async-start | bytes 2097152 | tf_op jit(solution)/shard_map/all_to_all | solution.py:248
  124.3 1.9 collective-permute-start.5
  126.2 3.3 %collective-permute-start.2 = (bf16[2,64,256]{2,1,0:T(8,128)(2,1)S(1)}, bf16[2,64,256]{2,1,0:T(8,128)(2,1)S(1)}, u32[]{:S(2)}, u32[]{:S(2)}) collective-permute-start(bf16[2,64,256]{2,1,0:T(8,128)(2,1)S(1)} %get-tuple-element.48), channel_id=1, source_target_pairs={{0,48},{16,0},{32,16},{48,32},{1,49},{17,1},{33,17},{49,33},{2,50}... | collective-permute-start | bytes 196616 | tf_op jit(solution)/shard_map/ppermute | solution.py:261
  129.6 4.2 %collective-permute-start.3 = (bf16[2,64,256]{2,1,0:T(8,128)(2,1)S(1)}, bf16[2,64,256]{2,1,0:T(8,128)(2,1)S(1)}, u32[]{:S(2)}, u32[]{:S(2)}) collective-permute-start(bf16[2,64,256]{2,1,0:T(8,128)(2,1)S(1)} %get-tuple-element.49), channel_id=1, source_target_pairs={{0,32},{16,48},{32,0},{48,16},{1,33},{17,49},{33,1},{49,17},{2,34}... | collective-permute-start | bytes 196616 | tf_op jit(solution)/shard_map/ppermute | solution.py:261
  133.8 3.4 %collective-permute-start.4 = (bf16[2,64,256]{2,1,0:T(8,128)(2,1)S(1)}, bf16[2,64,256]{2,1,0:T(8,128)(2,1)S(1)}, u32[]{:S(2)}, u32[]{:S(2)}) collective-permute-start(bf16[2,64,256]{2,1,0:T(8,128)(2,1)S(1)} %get-tuple-element.50), channel_id=1, source_target_pairs={{0,16},{16,32},{32,48},{48,0},{1,17},{17,33},{33,49},{49,1},{2,18}... | collective-permute-start | bytes 196616 | tf_op jit(solution)/shard_map/ppermute | solution.py:261
  137.2 6.5 %collective-permute-done.2 = bf16[2,64,256]{2,1,0:T(8,128)(2,1)S(1)} collective-permute-done((bf16[2,64,256]{2,1,0:T(8,128)(2,1)S(1)}, bf16[2,64,256]{2,1,0:T(8,128)(2,1)S(1)}, u32[]{:S(2)}, u32[]{:S(2)}) %collective-permute-start.2) | collective-permute-done | bytes 65568 | tf_op jit(solution)/shard_map/ppermute | solution.py:261
  143.7 8.2 %collective-permute-done.3 = bf16[2,64,256]{2,1,0:T(8,128)(2,1)S(1)} collective-permute-done((bf16[2,64,256]{2,1,0:T(8,128)(2,1)S(1)}, bf16[2,64,256]{2,1,0:T(8,128)(2,1)S(1)}, u32[]{:S(2)}, u32[]{:S(2)}) %collective-permute-start.3) | collective-permute-done | bytes 65568 | tf_op jit(solution)/shard_map/ppermute | solution.py:261
  152.0 1.0 all-to-all-done.2
  155.6 1.1 select_bitcast_fusion.1
  157.5 1.1 copy.90
  158.6 1.2 reshape.60
  160.3 1.1 copy.105
  161.3 1.9 collective-permute-start.7
  163.2 2.3 %collective-permute-done.7 = f32[32,42,128]{2,0,1:T(8,128)S(1)} collective-permute-done((f32[32,42,128]{2,0,1:T(8,128)}, f32[32,42,128]{2,0,1:T(8,128)S(1)}, u32[]{:S(2)}, u32[]{:S(2)}) %collective-permute-start.7) | collective-permute-done | bytes 688160 | tf_op jit(solution)/shard_map/ppermute | solution.py:252
  165.6 1.2 fusion.1
  166.7 10.6 %all-to-all-start.3 = ((bf16[32,42,128]{2,1,0:T(8,128)(2,1)}), bf16[32,42,128]{2,1,0:T(8,128)(2,1)S(1)}, u32[]{:S(2)}, u32[]{:S(2)}) async-start(bf16[32,42,128]{2,1,0:T(8,128)(2,1)} %fusion.1), calls=%async_computation.3 | async-start | bytes 786432 | tf_op jit(solution)/shard_map/all_to_all | solution.py:248
  177.5 2.0 copy-done.1
  179.5 4.3 %input_gradient.1 = bf16[128,2048]{1,0:T(8,128)(2,1)S(1)} custom-call(s32[2]{0:T(128)S(1)} %pad_add_fusion.place_ref, bf16[128,1024]{1,0:T(8,128)(2,1)S(1)} %bitcast.104, bf16[128,640]{1,0:T(8,128)(2,1)S(1)} %pad_maximum_fusion.4.rest_ref, bf16[8,4,32,1664]{3,2,1,0:T(8,128)(2,1)S(1)} %bitcast.107, bf16[8,4,32,1664]{3,2,1,0:T(8,128)(2,1)} %collective-permute-done.5.other_ref), custom_call_target="tpu_custom_call" | custom-call | tf_op jit(solution)/shard_map/input_gradient/pallas_call | solution.py:237
  183.8 2.5 %collective-permute-start.6 = (bf16[1,2,64,2048]{3,2,1,0:T(8,128)(2,1)S(1)}, bf16[1,2,64,2048]{3,2,1,0:T(8,128)(2,1)S(1)}, u32[]{:S(2)}, u32[]{:S(2)}) collective-permute-start(bf16[1,2,64,2048]{3,2,1,0:T(8,128)(2,1)S(1)} %bitcast.108), channel_id=1, source_target_pairs={{64,0},{128,64},{192,128},{256,192},{320,256},{384,320},{448,384},... | collective-permute-start | bytes 1572872 | tf_op jit(solution)/shard_map/ppermute | solution.py:257
  186.3 28.8 %collective-permute-done.6 = bf16[1,2,64,2048]{3,2,1,0:T(8,128)(2,1)S(1)} collective-permute-done((bf16[1,2,64,2048]{3,2,1,0:T(8,128)(2,1)S(1)}, bf16[1,2,64,2048]{3,2,1,0:T(8,128)(2,1)S(1)}, u32[]{:S(2)}, u32[]{:S(2)}) %collective-permute-start.6) | collective-permute-done | bytes 524320 | tf_op jit(solution)/shard_map/ppermute | solution.py:257
  216.5 0.8 copy.115
  (82 shorter events, 8.6 us)
Async XLA Ops:
  7.2 147.6 %copy-start = (bf16[1,2,64,2048]{3,2,1,0:T(8,128)(2,1)S(1)}, bf16[1,2,64,2048]{3,2,1,0:T(8,128)(2,1)}, u32[]{:S(2)}) copy-start(bf16[1,2,64,2048]{3,2,1,0:T(8,128)(2,1)} %param.8) | copy-start | bytes 1572868
  7.2 9.0 %copy-start.9 = (bf16[1,32,1536]{2,1,0:T(8,128)(2,1)S(1)}, bf16[1,32,1536]{2,1,0:T(8,128)(2,1)}, u32[]{:S(2)}) copy-start(bf16[1,32,1536]{2,1,0:T(8,128)(2,1)} %param.12) | copy-start | bytes 294916
  7.2 9.0 %copy-start.8 = (bf16[1,2,64,1024]{3,2,1,0:T(8,128)(2,1)S(1)}, bf16[1,2,64,1024]{3,2,1,0:T(8,128)(2,1)}, u32[]{:S(2)}) copy-start(bf16[1,2,64,1024]{3,2,1,0:T(8,128)(2,1)} %param.9) | copy-start | bytes 786436
  7.2 9.2 %copy-start.11 = (bf16[1,32,128]{2,1,0:T(8,128)(2,1)S(1)}, bf16[1,32,128]{2,1,0:T(8,128)(2,1)}, u32[]{:S(2)}) copy-start(bf16[1,32,128]{2,1,0:T(8,128)(2,1)} %param.14) | copy-start | bytes 24580
  9.1 7.4 %copy-start.3 = (bf16[1,2,64,2048]{3,2,1,0:T(8,128)(2,1)S(1)}, bf16[1,2,64,2048]{3,2,1,0:T(8,128)(2,1)}, u32[]{:S(2)}) copy-start(bf16[1,2,64,2048]{3,2,1,0:T(8,128)(2,1)} %param.11) | copy-start | bytes 1572868
  9.9 13.4 %all-to-all-start = ((bf16[8,128,128]{2,1,0:T(8,128)(2,1)}), bf16[8,128,128]{2,1,0:T(8,128)(2,1)S(1)}, u32[]{:S(2)}, u32[]{:S(2)}) async-start(bf16[8,128,128]{2,1,0:T(8,128)(2,1)} %bitcast.5), calls=%async_computation | async-start | bytes 524288 | tf_op jit(solution)/shard_map/all_to_all | solution.py:248
  16.2 56.3 %all-gather.5.cloned.1.call-start = ((), (), s32[]{:S(2)}) async-start(), calls=%async_computation.4 | async-start | bytes 2359296 | tf_op jit(solution)/shard_map/all_gather | solution.py:317
  23.3 0.7 copy-start.2
  24.1 100.3 %all-gather.7.cloned.1.call-start = ((), (), s32[]{:S(2)}) async-start(), calls=%async_computation.5 | async-start | bytes 3833856 | tf_op jit(solution)/shard_map/all_gather | solution.py:330
  72.5 5.7 %collective-permute-start = (bf16[4,64,3456]{2,1,0:T(8,128)(2,1)S(1)}, bf16[4,64,3456]{2,1,0:T(8,128)(2,1)}, u32[]{:S(2)}, u32[]{:S(2)}) collective-permute-start(bf16[4,64,3456]{2,1,0:T(8,128)(2,1)S(1)} %all_to_all.20.own_ref), channel_id=1, source_target_pairs={{0,1},{1,0},{2,3},{3,2},{4,5},{5,4},{6,7},{7,6},{8,9},{9,8},{10,11... | collective-permute-start | bytes 5308424 | tf_op jit(solution)/shard_map/ppermute | solution.py:252
  110.1 13.8 %collective-permute-start.1 = (bf16[4,64,256]{2,1,0:T(8,128)(2,1)S(1)}, bf16[4,64,256]{2,1,0:T(8,128)(2,1)S(1)}, u32[]{:S(2)}, u32[]{:S(2)}) collective-permute-start(bf16[4,64,256]{2,1,0:T(8,128)(2,1)S(1)} %slice_bitcast_fusion.3), channel_id=1, source_target_pairs={{0,1},{1,0},{2,3},{3,2},{4,5},{5,4},{6,7},{7,6},{8,9},{9,8},{10,11... | collective-permute-start | bytes 393224 | tf_op jit(solution)/shard_map/ppermute | solution.py:252
  112.1 40.8 %all-to-all-start.2 = ((bf16[64,64,128]{2,1,0:T(8,128)(2,1)}), bf16[64,64,128]{2,1,0:T(8,128)(2,1)S(1)}, u32[]{:S(2)}, u32[]{:S(2)}) async-start(bf16[64,64,128]{2,1,0:T(8,128)(2,1)} %bitcast.27), calls=%async_computation.2 | async-start | bytes 2097152 | tf_op jit(solution)/shard_map/all_to_all | solution.py:248
  124.0 29.9 %copy-start.10 = (bf16[1,64,1280]{2,1,0:T(8,128)(2,1)S(1)}, bf16[1,64,1280]{2,1,0:T(8,128)(2,1)}, u32[]{:S(2)}) copy-start(bf16[1,64,1280]{2,1,0:T(8,128)(2,1)} %param.15) | copy-start | bytes 491524
  124.3 31.3 %collective-permute-start.5 = (bf16[8,4,32,1664]{3,2,1,0:T(8,128)(2,1)}, bf16[8,4,32,1664]{3,2,1,0:T(8,128)(2,1)}, u32[]{:S(2)}, u32[]{:S(2)}) collective-permute-start(bf16[8,4,32,1664]{3,2,1,0:T(8,128)(2,1)} %bitcast.105), channel_id=1, source_target_pairs={{0,1},{1,0},{2,3},{3,2},{4,5},{5,4},{6,7},{7,6},{8,9},{9,8},{10,11... | collective-permute-start | bytes 10223624 | tf_op jit(solution)/shard_map/ppermute | solution.py:252
  126.2 17.5 %collective-permute-start.2 = (bf16[2,64,256]{2,1,0:T(8,128)(2,1)S(1)}, bf16[2,64,256]{2,1,0:T(8,128)(2,1)S(1)}, u32[]{:S(2)}, u32[]{:S(2)}) collective-permute-start(bf16[2,64,256]{2,1,0:T(8,128)(2,1)S(1)} %get-tuple-element.48), channel_id=1, source_target_pairs={{0,48},{16,0},{32,16},{48,32},{1,49},{17,1},{33,17},{49,33},{2,50}... | collective-permute-start | bytes 196616 | tf_op jit(solution)/shard_map/ppermute | solution.py:261
  129.6 22.4 %collective-permute-start.3 = (bf16[2,64,256]{2,1,0:T(8,128)(2,1)S(1)}, bf16[2,64,256]{2,1,0:T(8,128)(2,1)S(1)}, u32[]{:S(2)}, u32[]{:S(2)}) collective-permute-start(bf16[2,64,256]{2,1,0:T(8,128)(2,1)S(1)} %get-tuple-element.49), channel_id=1, source_target_pairs={{0,32},{16,48},{32,0},{48,16},{1,33},{17,49},{33,1},{49,17},{2,34}... | collective-permute-start | bytes 196616 | tf_op jit(solution)/shard_map/ppermute | solution.py:261
  133.8 18.2 %collective-permute-start.4 = (bf16[2,64,256]{2,1,0:T(8,128)(2,1)S(1)}, bf16[2,64,256]{2,1,0:T(8,128)(2,1)S(1)}, u32[]{:S(2)}, u32[]{:S(2)}) collective-permute-start(bf16[2,64,256]{2,1,0:T(8,128)(2,1)S(1)} %get-tuple-element.50), channel_id=1, source_target_pairs={{0,16},{16,32},{32,48},{48,0},{1,17},{17,33},{33,49},{49,1},{2,18}... | collective-permute-start | bytes 196616 | tf_op jit(solution)/shard_map/ppermute | solution.py:261
  154.1 1.1 copy-start.4
  154.8 0.8 copy-start.6
  160.2 17.1 %copy-start.5 = (bf16[128,64]{1,0:T(8,128)(2,1)S(1)}, bf16[128,64]{1,0:T(8,128)(2,1)}, u32[]{:S(2)}) copy-start(bf16[128,64]{1,0:T(8,128)(2,1)} %copy-done.4) | copy-start | bytes 49156
  160.3 17.1 %copy-start.7 = (bf16[128,64]{1,0:T(8,128)(2,1)S(1)}, bf16[128,64]{1,0:T(8,128)(2,1)}, u32[]{:S(2)}) copy-start(bf16[128,64]{1,0:T(8,128)(2,1)} %copy-done.6) | copy-start | bytes 49156
  161.3 4.2 %collective-permute-start.7 = (f32[32,42,128]{2,0,1:T(8,128)}, f32[32,42,128]{2,0,1:T(8,128)S(1)}, u32[]{:S(2)}, u32[]{:S(2)}) collective-permute-start(f32[32,42,128]{2,0,1:T(8,128)} %bitcast.97), channel_id=1, source_target_pairs={{0,1},{1,0},{2,3},{3,2},{4,5},{5,4},{6,7},{7,6},{8,9},{9,8},{10,11... | collective-permute-start | bytes 2064392 | tf_op jit(solution)/shard_map/ppermute | solution.py:252
  166.7 48.4 %all-to-all-start.3 = ((bf16[32,42,128]{2,1,0:T(8,128)(2,1)}), bf16[32,42,128]{2,1,0:T(8,128)(2,1)S(1)}, u32[]{:S(2)}, u32[]{:S(2)}) async-start(bf16[32,42,128]{2,1,0:T(8,128)(2,1)} %fusion.1), calls=%async_computation.3 | async-start | bytes 786432 | tf_op jit(solution)/shard_map/all_to_all | solution.py:248
  177.5 2.0 copy-start.1
  183.8 31.3 %collective-permute-start.6 = (bf16[1,2,64,2048]{3,2,1,0:T(8,128)(2,1)S(1)}, bf16[1,2,64,2048]{3,2,1,0:T(8,128)(2,1)S(1)}, u32[]{:S(2)}, u32[]{:S(2)}) collective-permute-start(bf16[1,2,64,2048]{3,2,1,0:T(8,128)(2,1)S(1)} %bitcast.108), channel_id=1, source_target_pairs={{64,0},{128,64},{192,128},{256,192},{320,256},{384,320},{448,384},... | collective-permute-start | bytes 1572872 | tf_op jit(solution)/shard_map/ppermute | solution.py:257
Sparse Core Ops, SparseCore 0:
  24.2 48.2 all-gather.4
  75.1 49.1 all-gather.6

commit v3 on v2

--- a/solution.py
+++ b/solution.py
@@ -165,9 +165,31 @@
     lax.fori_loop(0, LINE, finish, 0)
 
 
-def input_kernel(place_ref, query_ref, rest_ref, own_ref, other_ref, out_ref):
+def token_kernel(query_ref, kv_ref, query_up_ref, value_up_ref, pairs_ref, between_ref):
+    halves = LINE // SEQS
+    rows = []
+    for s in range(SEQS):
+        groups = []
+        for g in range(KEY_VALUE_HEADS):
+            first = ((s * halves + g // CORES) * RING) * CORES + g % CORES
+            total = kv_ref[first].astype(jnp.float32)
+            for z in range(1, RING):
+                total = total + kv_ref[first + z * CORES].astype(jnp.float32)
+            groups.append(total)
+        rows.append(jnp.concatenate(groups, axis=1))
+    pairs = jnp.concatenate(rows, axis=0).astype(jnp.bfloat16)
+    pairs_ref[...] = pairs
+    between_ref[...] = (
+        contract(query_ref[...], query_up_ref[...], ((1,), (1,)))
+        + contract(pairs, value_up_ref[...], ((1,), (1,)))
+    ).astype(jnp.bfloat16)
+
+
+def input_kernel(place_ref, query_ref, pairs_ref, between_ref, own_ref, other_ref, out_ref):
     core = place_ref[1]
-    query, rest = query_ref[...], rest_ref[...]
+    query, pairs = query_ref[...], pairs_ref[...]
+    scaled = between_ref[...] * jnp.bfloat16(ADAPTER_SCALE)
+    kv_end = WEIGHT_COLS - 2 * ADAPTER_RANK
     part = RING // 2
     for y in range(LINE):
         for half in range(2):
@@ -175,9 +197,11 @@
             own, other = own_ref[ring, y], other_ref[ring, y]
             weight = jnp.stack(
                 [jnp.where(core == 0, own, other), jnp.where(core == 0, other, own)], axis=1
-            ).reshape(part * CORES * WEIGHT_ROWS, -1)
-            product = contract(query, weight[:, :Q_COLS], ((1,), (1,))) + contract(
-                rest, weight[:, Q_COLS : Q_COLS + rest.shape[1]], ((1,), (1,))
+            ).reshape(part * CORES * WEIGHT_ROWS, WEIGHT_COLS)
+            product = (
+                contract(query, weight[:, :Q_COLS], ((1,), (1,)))
+                + contract(pairs, weight[:, Q_COLS:kv_end], ((1,), (1,)))
+                + contract(scaled, weight[:, kv_end:], ((1,), (1,)))
             )
             width = product.shape[1]
             at = (2 * y + half) * width
@@ -233,15 +257,33 @@
     )(terms)
 
 
-def input_product(place, query, rest, own, other):
+def token_gradients(query, kv_back, query_up, value_up):
+    tokens = query.shape[0]
+    return pl.pallas_call(
+        token_kernel,
+        out_shape=(
+            jax.ShapeDtypeStruct((tokens, KEY_VALUE_HEADS * KV_COLS), jnp.bfloat16),
+            jax.ShapeDtypeStruct((tokens, 2 * ADAPTER_RANK), jnp.bfloat16),
+        ),
+        in_specs=[VMEM] * 4,
+        out_specs=(VMEM, VMEM),
+        compiler_params=PARAMS,
+        cost_estimate=pl.CostEstimate(
+            flops=16 * 10**9, bytes_accessed=2 * 2**20, transcendentals=0
+        ),
+        name="token_gradients",
+    )(query, kv_back, query_up, value_up)
+
+
+def input_product(place, query, pairs, between, own, other):
     return pl.pallas_call(
         input_kernel,
         out_shape=jax.ShapeDtypeStruct((query.shape[0], MODEL_WIDTH), jnp.bfloat16),
-        in_specs=[SMEM] + [VMEM] * 4,
+        in_specs=[SMEM] + [VMEM] * 5,
         out_specs=VMEM,
         compiler_params=PARAMS,
         name="input_gradient",
-    )(place, query, rest, own, other)
+    )(place, query, pairs, between, own, other)
 
 
 def exchange(blocks, axes):
@@ -307,7 +349,15 @@
 
     grad_part = jnp.broadcast_to(out_grad[0][:, None], (SEQS, halves, PER_SEQ, MODEL_WIDTH))
     query_part = queries[0].reshape(SEQS, PER_SEQ, halves, PAIR_WIDTH).transpose(0, 2, 1, 3)
-    weights = jnp.concatenate([qkv_weight[0], adapter_down_maps[0]], axis=1)
+    kv_weight = (
+        qkv_weight[0, :, Q_COLS:]
+        .reshape(WEIGHT_ROWS, 2, KEY_VALUE_HEADS, HEAD_SIZE)
+        .transpose(0, 2, 1, 3)
+        .reshape(WEIGHT_ROWS, KEY_VALUE_HEADS * KV_COLS)
+    )
+    weights = jnp.concatenate(
+        [qkv_weight[0, :, :Q_COLS], kv_weight, adapter_down_maps[0]], axis=1
+    )
     folded = jnp.concatenate([weights[:, :FOLD], weights[:, WEIGHT_COLS - FOLD :]], axis=0)
     weight_part = jnp.broadcast_to(folded, (SEQS, halves, PER_SEQ, FOLD))
     row_send = jnp.concatenate([grad_part, query_part, weight_part], axis=3).reshape(
@@ -347,24 +397,18 @@
         .transpose(0, 2, 1, 3)
         .reshape(tokens, Q_COLS)
     )
-    kv_local = (
-        jnp.sum(
-            kv_back.reshape(SEQS, halves, RING, CORES, PER_SEQ, KV_COLS).astype(jnp.float32), axis=2
-        )
-        .astype(jnp.bfloat16)
-        .reshape(SEQS, KEY_VALUE_HEADS, PER_SEQ, 2, HEAD_SIZE)
-        .transpose(0, 2, 3, 1, 4)
-        .reshape(tokens, 2 * KEY_VALUE_HEADS * HEAD_SIZE)
-    )
-    value_local = kv_local[:, KEY_VALUE_HEADS * HEAD_SIZE :]
     up_maps = adapter_up_maps[0]
-    adapter_between = jnp.concatenate(
-        [
-            contract(query_local, up_maps[:, :Q_COLS], ((1,), (1,))),
-            contract(value_local, up_maps[:, Q_COLS:], ((1,), (1,))),
-        ],
-        axis=1,
-    ).astype(jnp.bfloat16)
+    query_up = jnp.pad(up_maps[:, :Q_COLS], ((0, ADAPTER_RANK), (0, 0)))
+    value_up = jnp.pad(
+        up_maps[:, Q_COLS:].reshape(ADAPTER_RANK, KEY_VALUE_HEADS, 1, HEAD_SIZE),
+        ((ADAPTER_RANK, 0), (0, 0), (1, 0), (0, 0)),
+    ).reshape(2 * ADAPTER_RANK, KEY_VALUE_HEADS * KV_COLS)
+    kv_local, adapter_between = token_gradients(query_local, kv_back, query_up, value_up)
+    input_gradient = input_product(
+        place, query_local, kv_local, adapter_between, weight_own, weight_other
+    )
+    passed = from_next(input_gradient.reshape(1, SEQS, PER_SEQ, MODEL_WIDTH))
+
     down_own, down_other = weight_own[..., qkv_cols:], weight_other[..., qkv_cols:]
     down_all = (
         core_order(down_own, down_other, core, 2)
@@ -375,26 +419,21 @@
     hidden_rows = hidden[0].reshape(tokens, MODEL_WIDTH)
     adapter_reduced = dot(hidden_rows, down_all).astype(jnp.bfloat16)
     a_term = contract(hidden_rows, adapter_between, ((0,), (0,)))
+    value_term = contract(kv_local, adapter_reduced[:, ADAPTER_RANK:], ((0,), (0,)))
+    value_term = value_term.reshape(KEY_VALUE_HEADS, 2, HEAD_SIZE, ADAPTER_RANK)[:, 1]
     b_turned = jnp.concatenate(
         [
             contract(query_local, adapter_reduced[:, :ADAPTER_RANK], ((0,), (0,))),
-            contract(value_local, adapter_reduced[:, ADAPTER_RANK:], ((0,), (0,))),
+            value_term.reshape(KEY_VALUE_HEADS * HEAD_SIZE, ADAPTER_RANK),
         ],
         axis=0,
     )
-    ranks = 2 * ADAPTER_RANK
-    a_send = a_term.reshape(LINE * RING, CORES, WEIGHT_ROWS, ranks)
-    b_send = b_turned.reshape(LINE * RING, CORES, 2, B_ROWS, ADAPTER_RANK)
-    b_send = jnp.concatenate([b_send[:, :, 0], b_send[:, :, 1]], axis=3)
-    term_send = jnp.concatenate([a_send, b_send], axis=2)
-    kept = lax.dynamic_index_in_dim(term_send, core, 1, keepdims=False)
-    given = lax.dynamic_index_in_dim(term_send, 1 - core, 1, keepdims=False)
-    term_chip = (kept + swap(given)).astype(jnp.bfloat16)
-    a_sum, b_sum = term_sums(exchange(term_chip, ("y", "z")))
-
-    rest = jnp.concatenate([kv_local, adapter_between * jnp.bfloat16(ADAPTER_SCALE)], axis=1)
-    input_gradient = input_product(place, query_local, rest, weight_own, weight_other)
-    passed = from_next(input_gradient.reshape(1, SEQS, PER_SEQ, MODEL_WIDTH))
+    a_send = a_term.astype(jnp.bfloat16).reshape(DEVICES, WEIGHT_ROWS, 2 * ADAPTER_RANK)
+    b_send = b_turned.astype(jnp.bfloat16).reshape(DEVICES, 2, B_ROWS, ADAPTER_RANK)
+    b_send = jnp.concatenate([b_send[:, 0], b_send[:, 1]], axis=2)
+    term_send = jnp.concatenate([a_send, b_send], axis=1)
+    a_sum, b_sum = term_sums(exchange(term_send, SEQ_AXES))
+
     return (passed, a_sum[None], b_sum[None])
 
 

time: 225 us -> 223 us (level)
  the two profiles are of different devices: /device:TPU:62 before, /device:TPU:6 now
where the time goes in v3:
time: 223 us; the launch traced here: 222 us
  waiting for transfers between devices  63.6 us (29%)
  starting transfers between devices  46.5 us (21%)
  blocking collectives  44.6 us (20%)
  Pallas kernels  37.2 us (17%)
  between operations  14.7 us (7%)
  local copies, waits for them, and re-layouts  8.83 us (4%)
  other arithmetic  5.25 us (2%)
    all_to_all x1, blocking collectives, exchange(): return lax.all_to_all(blocks, axes, split_axis=0, concat_axis=0, tiled=True)  44.6 us
    pallas_call x1, Pallas kernels, attend(): pl.pallas_call(attention_kernel, out_shape=(jax.ShapeDtypeStruct((LINE, C...  31.8 us
    all_to_all x3, starting transfers between devices, exchange(): return lax.all_to_all(blocks, axes, split_axis=0, concat_axis=0, tiled=True)  22.5 us
    ppermute x1, waiting for transfers between devices, from_next(): lax.ppermute(block, 'section', [((i + 1) % sections, i) for i in range(se...  21.4 us
    ppermute x3, waiting for transfers between devices, along(): lax.ppermute(block, 'y', [(y, (y + distance) % LINE) for y in range(LINE)])  18.7 us
    all_to_all x3, waiting for transfers between devices, exchange(): return lax.all_to_all(blocks, axes, split_axis=0, concat_axis=0, tiled=True)  17.4 us
    ppermute x3, starting transfers between devices, along(): lax.ppermute(block, 'y', [(y, (y + distance) % LINE) for y in range(LINE)])  10.3 us
    ppermute x1, starting transfers between devices, from_next(): lax.ppermute(block, 'section', [((i + 1) % sections, i) for i in range(se...  7.54 us
  transfers between devices with their start and end apart: 12, of which 7 were waited for; matrix products, arithmetic and copies ran while one was open for 2% of the time, Pallas kernels for 16%

profile of v3, /device:TPU:6, one launch (start us, length us, event | category | flops | bytes accessed | tf_op | source)
XLA Modules:
  0.0 221.7 jit_solution(5225855742833646739)
XLA Ops:
  7.2 0.9 reshape_squeeze.20
  8.2 0.9 reshape_squeeze.19
  9.2 0.7 pad_maximum_fusion.2
  9.9 4.9 %all-to-all-start = ((bf16[8,128,128]{2,1,0:T(8,128)(2,1)}), bf16[8,128,128]{2,1,0:T(8,128)(2,1)S(1)}, u32[]{:S(2)}, u32[]{:S(2)}) async-start(bf16[8,128,128]{2,1,0:T(8,128)(2,1)} %bitcast.5), calls=%async_computation | async-start | bytes 524288 | tf_op jit(solution)/shard_map/all_to_all | solution.py:290
  15.6 1.4 pad_maximum_fusion
  17.0 7.6 %all-to-all-done = bf16[8,128,128]{2,1,0:T(8,128)(2,1)S(1)} async-done(((bf16[8,128,128]{2,1,0:T(8,128)(2,1)}), bf16[8,128,128]{2,1,0:T(8,128)(2,1)S(1)}, u32[]{:S(2)}, u32[]{:S(2)}) %all-to-all-start) | async-done | bytes 262176 | tf_op jit(solution)/shard_map/all_to_all | solution.py:290
  24.5 0.7 copy-done.2
  25.3 44.6 %all_to_all.20.own_ref = bf16[4,64,3456]{2,1,0:T(8,128)(2,1)S(1)} all-to-all(bf16[4,64,3456]{2,1,0:T(8,128)(2,1)} %bitcast.108), channel_id=1, replica_groups=mesh['section'=8,'y'=4,'z'=8,'core'=2] {'y'}, dimensions={0} | all-to-all | bytes 3538944 | tf_op jit(solution)/shard_map/all_to_all | solution.py:290
  70.0 0.8 pad_maximum_fusion.1
  70.8 2.3 %all-gather.5.cloned.1.call-done = bf16[64,128,128]{2,1,0:T(8,128)(2,1)} async-done(((bf16[8,128,128]{2,1,0:T(8,128)(2,1)}), bf16[64,128,128]{2,1,0:T(8,128)(2,1)}) %all-gather.5.cloned.1.call-update) | async-done | bytes 2097168 | tf_op jit(solution)/shard_map/all_gather | solution.py:367
  73.1 1.9 collective-permute-start
  75.2 3.7 %collective-permute-done.other_ref = bf16[4,64,3456]{2,1,0:T(8,128)(2,1)} collective-permute-done((bf16[4,64,3456]{2,1,0:T(8,128)(2,1)S(1)}, bf16[4,64,3456]{2,1,0:T(8,128)(2,1)}, u32[]{:S(2)}, u32[]{:S(2)}) %collective-permute-start) | collective-permute-done | bytes 1769504 | tf_op jit(solution)/shard_map/ppermute | solution.py:294
  78.9 31.8 %attention.1 = (bf16[4,2,64,256]{3,2,1,0:T(8,128)(2,1)S(1)}, bf16[4,16,64,128]{3,2,1,0:T(8,128)(2,1)}) custom-call(s32[2]{0:T(128)S(1)} %pad_add_fusion.place_ref, bf16[4,64,3456]{2,1,0:T(8,128)(2,1)S(1)} %all_to_all.20.own_ref, bf16[4,64,3456]{2,1,0:T(8,128)(2,1)} %collective-permute-done.other_ref, bf16[8,4,2,128,128]{4,3,2,1,0:T(8,128)(2,1)} %bitcast.109), custom_call_target="tpu_custom_call" | custom-call | tf_op jit(solution)/shard_map/attention/pallas_call | solution.py:227
  110.7 2.2 collective-permute-start.1
  113.0 9.9 %all-to-all-start.2 = ((bf16[64,64,128]{2,1,0:T(8,128)(2,1)}), bf16[64,64,128]{2,1,0:T(8,128)(2,1)S(1)}, u32[]{:S(2)}, u32[]{:S(2)}) async-start(bf16[64,64,128]{2,1,0:T(8,128)(2,1)} %bitcast.28), calls=%async_computation.2 | async-start | bytes 2097152 | tf_op jit(solution)/shard_map/all_to_all | solution.py:290
  123.0 5.5 %collective-permute-start.2 = (bf16[2,64,256]{2,1,0:T(8,128)(2,1)S(1)}, bf16[2,64,256]{2,1,0:T(8,128)(2,1)S(1)}, u32[]{:S(2)}, u32[]{:S(2)}) collective-permute-start(bf16[2,64,256]{2,1,0:T(8,128)(2,1)S(1)} %get-tuple-element.46), channel_id=1, source_target_pairs={{0,48},{16,0},{32,16},{48,32},{1,49},{17,1},{33,17},{49,33},{2,50}... | collective-permute-start | bytes 196616 | tf_op jit(solution)/shard_map/ppermute | solution.py:303
  128.9 1.9 collective-permute-start.3
  130.8 2.9 %collective-permute-start.4 = (bf16[2,64,256]{2,1,0:T(8,128)(2,1)S(1)}, bf16[2,64,256]{2,1,0:T(8,128)(2,1)S(1)}, u32[]{:S(2)}, u32[]{:S(2)}) collective-permute-start(bf16[2,64,256]{2,1,0:T(8,128)(2,1)S(1)} %get-tuple-element.48), channel_id=1, source_target_pairs={{0,16},{16,32},{32,48},{48,0},{1,17},{17,33},{33,49},{49,1},{2,18}... | collective-permute-start | bytes 196616 | tf_op jit(solution)/shard_map/ppermute | solution.py:303
  133.8 1.9 collective-permute-start.5
  135.7 8.6 %collective-permute-done.2 = bf16[2,64,256]{2,1,0:T(8,128)(2,1)S(1)} collective-permute-done((bf16[2,64,256]{2,1,0:T(8,128)(2,1)S(1)}, bf16[2,64,256]{2,1,0:T(8,128)(2,1)S(1)}, u32[]{:S(2)}, u32[]{:S(2)}) %collective-permute-start.2) | collective-permute-done | bytes 65568 | tf_op jit(solution)/shard_map/ppermute | solution.py:303
  144.4 10.0 %collective-permute-done.3 = bf16[2,64,256]{2,1,0:T(8,128)(2,1)S(1)} collective-permute-done((bf16[2,64,256]{2,1,0:T(8,128)(2,1)S(1)}, bf16[2,64,256]{2,1,0:T(8,128)(2,1)S(1)}, u32[]{:S(2)}, u32[]{:S(2)}) %collective-permute-start.3) | collective-permute-done | bytes 65568 | tf_op jit(solution)/shard_map/ppermute | solution.py:303
  155.7 1.1 select_bitcast_fusion.1
  158.7 1.1 maximum_maximum_fusion
  159.8 7.7 %all-to-all-start.3 = ((bf16[64,42,128]{2,1,0:T(8,128)(2,1)}), bf16[64,42,128]{2,1,0:T(8,128)(2,1)S(1)}, u32[]{:S(2)}, u32[]{:S(2)}) async-start(bf16[64,42,128]{2,1,0:T(8,128)(2,1)} %maximum_maximum_fusion), calls=%async_computation.3 | async-start | bytes 1572864 | tf_op jit(solution)/shard_map/all_to_all | solution.py:290
  167.5 2.0 copy-done.1
  169.5 4.3 %input_gradient.1 = bf16[128,2048]{1,0:T(8,128)(2,1)S(1)} custom-call(s32[2]{0:T(128)S(1)} %pad_add_fusion.place_ref, bf16[128,1024]{1,0:T(8,128)(2,1)S(1)} %bitcast.105, bf16[128,512]{1,0:T(8,128)(2,1)S(1)} %get-tuple-element.22.pairs_ref, bf16[128,128]{1,0:T(8,128)(2,1)S(1)} %get-tuple-element.23.between_ref, bf16[8,4,32,1664]{3,2,1,0:T(8,128)(2,1)S(1)} %bitcast.102, ...), custom_call_target="tpu_custom_call" | custom-call | tf_op jit(solution)/shard_map/input_gradient/pallas_call | solution.py:279
  173.8 7.5 %collective-permute-start.6 = (bf16[1,2,64,2048]{3,2,1,0:T(8,128)(2,1)S(1)}, bf16[1,2,64,2048]{3,2,1,0:T(8,128)(2,1)S(1)}, u32[]{:S(2)}, u32[]{:S(2)}) collective-permute-start(bf16[1,2,64,2048]{3,2,1,0:T(8,128)(2,1)S(1)} %bitcast.106), channel_id=1, source_target_pairs={{64,0},{128,64},{192,128},{256,192},{320,256},{384,320},{448,384},... | collective-permute-start | bytes 1572872 | tf_op jit(solution)/shard_map/ppermute | solution.py:299
  181.3 21.4 %collective-permute-done.6 = bf16[1,2,64,2048]{3,2,1,0:T(8,128)(2,1)S(1)} collective-permute-done((bf16[1,2,64,2048]{3,2,1,0:T(8,128)(2,1)S(1)}, bf16[1,2,64,2048]{3,2,1,0:T(8,128)(2,1)S(1)}, u32[]{:S(2)}, u32[]{:S(2)}) %collective-permute-start.6) | collective-permute-done | bytes 524320 | tf_op jit(solution)/shard_map/ppermute | solution.py:299
  202.8 9.8 %all-to-all-done.3.terms_ref = bf16[64,42,128]{2,1,0:T(8,128)(2,1)S(1)} async-done(((bf16[64,42,128]{2,1,0:T(8,128)(2,1)}), bf16[64,42,128]{2,1,0:T(8,128)(2,1)S(1)}, u32[]{:S(2)}, u32[]{:S(2)}) %all-to-all-start.3) | async-done | bytes 688160 | tf_op jit(solution)/shard_map/all_to_all | solution.py:290
  212.6 0.8 term_sums.1
  213.4 0.7 copy.64
  214.1 0.8 copy.83
  (75 shorter events, 4.5 us)
Async XLA Ops:
  7.2 147.9 %copy-start = (bf16[1,2,64,2048]{3,2,1,0:T(8,128)(2,1)S(1)}, bf16[1,2,64,2048]{3,2,1,0:T(8,128)(2,1)}, u32[]{:S(2)}) copy-start(bf16[1,2,64,2048]{3,2,1,0:T(8,128)(2,1)} %param.8) | copy-start | bytes 1572868
  7.2 7.7 %copy-start.6 = (bf16[1,32,1536]{2,1,0:T(8,128)(2,1)S(1)}, bf16[1,32,1536]{2,1,0:T(8,128)(2,1)}, u32[]{:S(2)}) copy-start(bf16[1,32,1536]{2,1,0:T(8,128)(2,1)} %param.12) | copy-start | bytes 294916
  7.2 7.7 %slice-start = ((bf16[1,32,1536]{2,1,0:T(8,128)(2,1)}), bf16[1,32,512]{2,1,0:T(8,128)(2,1)S(1)}, s32[]{:S(2)}) async-start(bf16[1,32,1536]{2,1,0:T(8,128)(2,1)} %param.12), calls=%async_computation.6 | async-start | bytes 65536 | tf_op jit(solution)/shard_map/slice | solution.py:353
  7.2 8.0 %copy-start.4 = (bf16[1,2,64,1024]{3,2,1,0:T(8,128)(2,1)S(1)}, bf16[1,2,64,1024]{3,2,1,0:T(8,128)(2,1)}, u32[]{:S(2)}) copy-start(bf16[1,2,64,1024]{3,2,1,0:T(8,128)(2,1)} %param.9) | copy-start | bytes 786436
  8.2 7.2 %copy-start.7 = (bf16[1,32,128]{2,1,0:T(8,128)(2,1)S(1)}, bf16[1,32,128]{2,1,0:T(8,128)(2,1)}, u32[]{:S(2)}) copy-start(bf16[1,32,128]{2,1,0:T(8,128)(2,1)} %param.14) | copy-start | bytes 24580
  9.2 6.3 %copy-start.3 = (bf16[1,2,64,2048]{3,2,1,0:T(8,128)(2,1)S(1)}, bf16[1,2,64,2048]{3,2,1,0:T(8,128)(2,1)}, u32[]{:S(2)}) copy-start(bf16[1,2,64,2048]{3,2,1,0:T(8,128)(2,1)} %param.11) | copy-start | bytes 1572868
  9.9 14.6 %all-to-all-start = ((bf16[8,128,128]{2,1,0:T(8,128)(2,1)}), bf16[8,128,128]{2,1,0:T(8,128)(2,1)S(1)}, u32[]{:S(2)}, u32[]{:S(2)}) async-start(bf16[8,128,128]{2,1,0:T(8,128)(2,1)} %bitcast.5), calls=%async_computation | async-start | bytes 524288 | tf_op jit(solution)/shard_map/all_to_all | solution.py:290
  14.8 58.3 %all-gather.5.cloned.1.call-start = ((), (), s32[]{:S(2)}) async-start(), calls=%async_computation.4 | async-start | bytes 2359296 | tf_op jit(solution)/shard_map/all_gather | solution.py:367
  24.5 0.7 copy-start.2
  25.3 108.5 %all-gather.7.cloned.1.call-start = ((), (), s32[]{:S(2)}) async-start(), calls=%async_computation.5 | async-start | bytes 3833856 | tf_op jit(solution)/shard_map/all_gather | solution.py:380
  73.1 5.7 %collective-permute-start = (bf16[4,64,3456]{2,1,0:T(8,128)(2,1)S(1)}, bf16[4,64,3456]{2,1,0:T(8,128)(2,1)}, u32[]{:S(2)}, u32[]{:S(2)}) collective-permute-start(bf16[4,64,3456]{2,1,0:T(8,128)(2,1)S(1)} %all_to_all.20.own_ref), channel_id=1, source_target_pairs={{0,1},{1,0},{2,3},{3,2},{4,5},{5,4},{6,7},{7,6},{8,9},{9,8},{10,11... | collective-permute-start | bytes 5308424 | tf_op jit(solution)/shard_map/ppermute | solution.py:294
  110.7 17.8 %copy-start.5 = (bf16[1,64,1280]{2,1,0:T(8,128)(2,1)S(1)}, bf16[1,64,1280]{2,1,0:T(8,128)(2,1)}, u32[]{:S(2)}) copy-start(bf16[1,64,1280]{2,1,0:T(8,128)(2,1)} %param.15) | copy-start | bytes 491524
  110.7 12.2 %collective-permute-start.1 = (bf16[4,64,256]{2,1,0:T(8,128)(2,1)S(1)}, bf16[4,64,256]{2,1,0:T(8,128)(2,1)S(1)}, u32[]{:S(2)}, u32[]{:S(2)}) collective-permute-start(bf16[4,64,256]{2,1,0:T(8,128)(2,1)S(1)} %slice_bitcast_fusion.3), channel_id=1, source_target_pairs={{0,1},{1,0},{2,3},{3,2},{4,5},{5,4},{6,7},{7,6},{8,9},{9,8},{10,11... | collective-permute-start | bytes 393224 | tf_op jit(solution)/shard_map/ppermute | solution.py:294
  113.0 41.8 %all-to-all-start.2 = ((bf16[64,64,128]{2,1,0:T(8,128)(2,1)}), bf16[64,64,128]{2,1,0:T(8,128)(2,1)S(1)}, u32[]{:S(2)}, u32[]{:S(2)}) async-start(bf16[64,64,128]{2,1,0:T(8,128)(2,1)} %bitcast.28), calls=%async_computation.2 | async-start | bytes 2097152 | tf_op jit(solution)/shard_map/all_to_all | solution.py:290
  123.0 21.3 %collective-permute-start.2 = (bf16[2,64,256]{2,1,0:T(8,128)(2,1)S(1)}, bf16[2,64,256]{2,1,0:T(8,128)(2,1)S(1)}, u32[]{:S(2)}, u32[]{:S(2)}) collective-permute-start(bf16[2,64,256]{2,1,0:T(8,128)(2,1)S(1)} %get-tuple-element.46), channel_id=1, source_target_pairs={{0,48},{16,0},{32,16},{48,32},{1,49},{17,1},{33,17},{49,33},{2,50}... | collective-permute-start | bytes 196616 | tf_op jit(solution)/shard_map/ppermute | solution.py:303
  128.9 25.5 %collective-permute-start.3 = (bf16[2,64,256]{2,1,0:T(8,128)(2,1)S(1)}, bf16[2,64,256]{2,1,0:T(8,128)(2,1)S(1)}, u32[]{:S(2)}, u32[]{:S(2)}) collective-permute-start(bf16[2,64,256]{2,1,0:T(8,128)(2,1)S(1)} %get-tuple-element.47), channel_id=1, source_target_pairs={{0,32},{16,48},{32,0},{48,16},{1,33},{17,49},{33,1},{49,17},{2,34}... | collective-permute-start | bytes 196616 | tf_op jit(solution)/shard_map/ppermute | solution.py:303
  130.8 23.6 %collective-permute-start.4 = (bf16[2,64,256]{2,1,0:T(8,128)(2,1)S(1)}, bf16[2,64,256]{2,1,0:T(8,128)(2,1)S(1)}, u32[]{:S(2)}, u32[]{:S(2)}) collective-permute-start(bf16[2,64,256]{2,1,0:T(8,128)(2,1)S(1)} %get-tuple-element.48), channel_id=1, source_target_pairs={{0,16},{16,32},{32,48},{48,0},{1,17},{17,33},{33,49},{49,1},{2,18}... | collective-permute-start | bytes 196616 | tf_op jit(solution)/shard_map/ppermute | solution.py:303
  133.8 21.9 %collective-permute-start.5 = (bf16[8,4,32,1664]{3,2,1,0:T(8,128)(2,1)}, bf16[8,4,32,1664]{3,2,1,0:T(8,128)(2,1)}, u32[]{:S(2)}, u32[]{:S(2)}) collective-permute-start(bf16[8,4,32,1664]{3,2,1,0:T(8,128)(2,1)} %bitcast.100), channel_id=1, source_target_pairs={{0,1},{1,0},{2,3},{3,2},{4,5},{5,4},{6,7},{7,6},{8,9},{9,8},{10,11... | collective-permute-start | bytes 10223624 | tf_op jit(solution)/shard_map/ppermute | solution.py:294
  159.8 52.8 %all-to-all-start.3 = ((bf16[64,42,128]{2,1,0:T(8,128)(2,1)}), bf16[64,42,128]{2,1,0:T(8,128)(2,1)S(1)}, u32[]{:S(2)}, u32[]{:S(2)}) async-start(bf16[64,42,128]{2,1,0:T(8,128)(2,1)} %maximum_maximum_fusion), calls=%async_computation.3 | async-start | bytes 1572864 | tf_op jit(solution)/shard_map/all_to_all | solution.py:290
  167.5 2.0 copy-start.1
  173.8 29.0 %collective-permute-start.6 = (bf16[1,2,64,2048]{3,2,1,0:T(8,128)(2,1)S(1)}, bf16[1,2,64,2048]{3,2,1,0:T(8,128)(2,1)S(1)}, u32[]{:S(2)}, u32[]{:S(2)}) collective-permute-start(bf16[1,2,64,2048]{3,2,1,0:T(8,128)(2,1)S(1)} %bitcast.106), channel_id=1, source_target_pairs={{64,0},{128,64},{192,128},{256,192},{320,256},{384,320},{448,384},... | collective-permute-start | bytes 1572872 | tf_op jit(solution)/shard_map/ppermute | solution.py:299
Sparse Core Ops, SparseCore 0:
  25.4 47.6 all-gather.4
  75.8 49.1 all-gather.6

commit v4 on v3

--- a/solution.py
+++ b/solution.py
@@ -407,7 +407,6 @@
     input_gradient = input_product(
         place, query_local, kv_local, adapter_between, weight_own, weight_other
     )
-    passed = from_next(input_gradient.reshape(1, SEQS, PER_SEQ, MODEL_WIDTH))
 
     down_own, down_other = weight_own[..., qkv_cols:], weight_other[..., qkv_cols:]
     down_all = (
@@ -428,12 +427,17 @@
         ],
         axis=0,
     )
-    a_send = a_term.astype(jnp.bfloat16).reshape(DEVICES, WEIGHT_ROWS, 2 * ADAPTER_RANK)
-    b_send = b_turned.astype(jnp.bfloat16).reshape(DEVICES, 2, B_ROWS, ADAPTER_RANK)
-    b_send = jnp.concatenate([b_send[:, 0], b_send[:, 1]], axis=2)
-    term_send = jnp.concatenate([a_send, b_send], axis=1)
-    a_sum, b_sum = term_sums(exchange(term_send, SEQ_AXES))
-
+    a_send = a_term.reshape(LINE * RING, CORES, WEIGHT_ROWS, 2 * ADAPTER_RANK)
+    b_send = b_turned.reshape(LINE * RING, CORES, 2, B_ROWS, ADAPTER_RANK)
+    b_send = jnp.concatenate([b_send[:, :, 0], b_send[:, :, 1]], axis=3)
+    term_send = jnp.concatenate([a_send, b_send], axis=2)
+    kept = lax.dynamic_index_in_dim(term_send, core, 1, keepdims=False)
+    given = lax.dynamic_index_in_dim(term_send, 1 - core, 1, keepdims=False)
+    taken = swap(given)
+    input_gradient, taken = ordered(input_gradient, taken)
+    passed = from_next(input_gradient.reshape(1, SEQS, PER_SEQ, MODEL_WIDTH))
+    term_chip = (kept + taken).astype(jnp.bfloat16)
+    a_sum, b_sum = term_sums(exchange(term_chip, ("y", "z")))
     return (passed, a_sum[None], b_sum[None])
 
 

time: 223 us -> 227 us (1.018)
  local copies, waits for them, and re-layouts: 8.83 us -> 12.2 us
    ppermute x3 -> x4, starting transfers between devices: 6.01 us -> 8.12 us  [swap(): return lax.ppermute(block, 'core', [(0, 1), (1, 0)])]
    unnamed x25 -> x29, local copies, waits for them, and re-layouts: 4.22 us -> 5.47 us
  transfers between devices with their start and end apart: 12 -> 13, of which waited for: 7 -> 7; matrix products, arithmetic and copies ran while one was open for 2% -> 2% of each run, Pallas kernels for 16% -> 16%
where the time goes in v4:
time: 227 us; the launch traced here: 225 us
  waiting for transfers between devices  61.6 us (27%)
  starting transfers between devices  48 us (21%)
  blocking collectives  44.6 us (20%)
  Pallas kernels  37.3 us (16%)
  between operations  14.7 us (6%)
  local copies, waits for them, and re-layouts  12.2 us (5%)
  other arithmetic  5.67 us (2%)
    all_to_all x1, blocking collectives, exchange(): return lax.all_to_all(blocks, axes, split_axis=0, concat_axis=0, tiled=True)  44.6 us
    pallas_call x1, Pallas kernels, attend(): pl.pallas_call(attention_kernel, out_shape=(jax.ShapeDtypeStruct((LINE, C...  31.8 us
    all_to_all x3, starting transfers between devices, exchange(): return lax.all_to_all(blocks, axes, split_axis=0, concat_axis=0, tiled=True)  21.9 us
    ppermute x1, waiting for transfers between devices, from_next(): lax.ppermute(block, 'section', [((i + 1) % sections, i) for i in range(se...  20.1 us
    ppermute x3, waiting for transfers between devices, along(): lax.ppermute(block, 'y', [(y, (y + distance) % LINE) for y in range(LINE)])  18.7 us
    all_to_all x3, waiting for transfers between devices, exchange(): return lax.all_to_all(blocks, axes, split_axis=0, concat_axis=0, tiled=True)  16.8 us
    ppermute x3, starting transfers between devices, along(): lax.ppermute(block, 'y', [(y, (y + distance) % LINE) for y in range(LINE)])  10.3 us
    ppermute x4, starting transfers between devices, swap(): return lax.ppermute(block, 'core', [(0, 1), (1, 0)])  8.12 us
  transfers between devices with their start and end apart: 13, of which 7 were waited for; matrix products, arithmetic and copies ran while one was open for 2% of the time, Pallas kernels for 16%

profile of v4, /device:TPU:6, one launch (start us, length us, event | category | flops | bytes accessed | tf_op | source)
XLA Modules:
  0.0 225.2 jit_solution(8526454748367467429)
XLA Ops:
  7.2 0.9 reshape_squeeze.19
  8.2 0.9 reshape_squeeze.18
  9.9 4.9 %all-to-all-start = ((bf16[8,128,128]{2,1,0:T(8,128)(2,1)}), bf16[8,128,128]{2,1,0:T(8,128)(2,1)S(1)}, u32[]{:S(2)}, u32[]{:S(2)}) async-start(bf16[8,128,128]{2,1,0:T(8,128)(2,1)} %bitcast.5), calls=%async_computation | async-start | bytes 524288 | tf_op jit(solution)/shard_map/all_to_all | solution.py:290
  15.6 1.4 pad_maximum_fusion
  17.0 7.6 %all-to-all-done = bf16[8,128,128]{2,1,0:T(8,128)(2,1)S(1)} async-done(((bf16[8,128,128]{2,1,0:T(8,128)(2,1)}), bf16[8,128,128]{2,1,0:T(8,128)(2,1)S(1)}, u32[]{:S(2)}, u32[]{:S(2)}) %all-to-all-start) | async-done | bytes 262176 | tf_op jit(solution)/shard_map/all_to_all | solution.py:290
  25.3 44.6 %all_to_all.20.own_ref = bf16[4,64,3456]{2,1,0:T(8,128)(2,1)S(1)} all-to-all(bf16[4,64,3456]{2,1,0:T(8,128)(2,1)} %bitcast.116), channel_id=1, replica_groups=mesh['section'=8,'y'=4,'z'=8,'core'=2] {'y'}, dimensions={0} | all-to-all | bytes 3538944 | tf_op jit(solution)/shard_map/all_to_all | solution.py:290
  70.0 0.8 pad_maximum_fusion.1
  70.8 2.3 %all-gather.5.cloned.1.call-done = bf16[64,128,128]{2,1,0:T(8,128)(2,1)} async-done(((bf16[8,128,128]{2,1,0:T(8,128)(2,1)}), bf16[64,128,128]{2,1,0:T(8,128)(2,1)}) %all-gather.5.cloned.1.call-update) | async-done | bytes 2097168 | tf_op jit(solution)/shard_map/all_gather | solution.py:367
  73.2 1.9 collective-permute-start
  75.2 3.7 %collective-permute-done.other_ref = bf16[4,64,3456]{2,1,0:T(8,128)(2,1)} collective-permute-done((bf16[4,64,3456]{2,1,0:T(8,128)(2,1)S(1)}, bf16[4,64,3456]{2,1,0:T(8,128)(2,1)}, u32[]{:S(2)}, u32[]{:S(2)}) %collective-permute-start) | collective-permute-done | bytes 1769504 | tf_op jit(solution)/shard_map/ppermute | solution.py:294
  78.9 31.8 %attention.1 = (bf16[4,2,64,256]{3,2,1,0:T(8,128)(2,1)S(1)}, bf16[4,16,64,128]{3,2,1,0:T(8,128)(2,1)}) custom-call(s32[2]{0:T(128)S(1)} %pad_add_fusion.place_ref, bf16[4,64,3456]{2,1,0:T(8,128)(2,1)S(1)} %all_to_all.20.own_ref, bf16[4,64,3456]{2,1,0:T(8,128)(2,1)} %collective-permute-done.other_ref, bf16[8,4,2,128,128]{4,3,2,1,0:T(8,128)(2,1)} %bitcast.118), custom_call_target="tpu_custom_call" | custom-call | tf_op jit(solution)/shard_map/attention/pallas_call | solution.py:227
  110.7 2.2 collective-permute-start.1
  113.0 9.9 %all-to-all-start.2 = ((bf16[64,64,128]{2,1,0:T(8,128)(2,1)}), bf16[64,64,128]{2,1,0:T(8,128)(2,1)S(1)}, u32[]{:S(2)}, u32[]{:S(2)}) async-start(bf16[64,64,128]{2,1,0:T(8,128)(2,1)} %bitcast.28), calls=%async_computation.2 | async-start | bytes 2097152 | tf_op jit(solution)/shard_map/all_to_all | solution.py:290
  123.0 5.5 %collective-permute-start.2 = (bf16[2,64,256]{2,1,0:T(8,128)(2,1)S(1)}, bf16[2,64,256]{2,1,0:T(8,128)(2,1)S(1)}, u32[]{:S(2)}, u32[]{:S(2)}) collective-permute-start(bf16[2,64,256]{2,1,0:T(8,128)(2,1)S(1)} %get-tuple-element.53), channel_id=1, source_target_pairs={{0,48},{16,0},{32,16},{48,32},{1,49},{17,1},{33,17},{49,33},{2,50}... | collective-permute-start | bytes 196616 | tf_op jit(solution)/shard_map/ppermute | solution.py:303
  128.9 1.9 collective-permute-start.3
  130.9 2.9 %collective-permute-start.4 = (bf16[2,64,256]{2,1,0:T(8,128)(2,1)S(1)}, bf16[2,64,256]{2,1,0:T(8,128)(2,1)S(1)}, u32[]{:S(2)}, u32[]{:S(2)}) collective-permute-start(bf16[2,64,256]{2,1,0:T(8,128)(2,1)S(1)} %get-tuple-element.55), channel_id=1, source_target_pairs={{0,16},{16,32},{32,48},{48,0},{1,17},{17,33},{33,49},{49,1},{2,18}... | collective-permute-start | bytes 196616 | tf_op jit(solution)/shard_map/ppermute | solution.py:303
  133.8 1.9 collective-permute-start.5
  135.7 8.6 %collective-permute-done.2 = bf16[2,64,256]{2,1,0:T(8,128)(2,1)S(1)} collective-permute-done((bf16[2,64,256]{2,1,0:T(8,128)(2,1)S(1)}, bf16[2,64,256]{2,1,0:T(8,128)(2,1)S(1)}, u32[]{:S(2)}, u32[]{:S(2)}) %collective-permute-start.2) | collective-permute-done | bytes 65568 | tf_op jit(solution)/shard_map/ppermute | solution.py:303
  144.4 10.0 %collective-permute-done.3 = bf16[2,64,256]{2,1,0:T(8,128)(2,1)S(1)} collective-permute-done((bf16[2,64,256]{2,1,0:T(8,128)(2,1)S(1)}, bf16[2,64,256]{2,1,0:T(8,128)(2,1)S(1)}, u32[]{:S(2)}, u32[]{:S(2)}) %collective-permute-start.3) | collective-permute-done | bytes 65568 | tf_op jit(solution)/shard_map/ppermute | solution.py:303
  155.8 1.1 select_bitcast_fusion.1
  158.2 1.1 copy.79
  159.3 1.2 reshape.63
  160.9 1.2 copy-done.2
  162.4 2.1 collective-permute-start.6
  164.5 2.0 copy-done.1
  166.5 4.4 %input_gradient.1 = bf16[128,2048]{1,0:T(8,128)(2,1)S(1)} custom-call(s32[2]{0:T(128)S(1)} %pad_add_fusion.place_ref, bf16[128,1024]{1,0:T(8,128)(2,1)S(1)} %bitcast.113, bf16[128,512]{1,0:T(8,128)(2,1)S(1)} %get-tuple-element.24.pairs_ref, bf16[128,128]{1,0:T(8,128)(2,1)S(1)} %get-tuple-element.25.between_ref, bf16[8,4,32,1664]{3,2,1,0:T(8,128)(2,1)S(1)} %bitcast.110, ...), custom_call_target="tpu_custom_call" | custom-call | tf_op jit(solution)/shard_map/input_gradient/pallas_call | solution.py:279
  171.0 1.2 fusion.1
  172.1 7.1 %all-to-all-start.3 = ((bf16[32,42,128]{2,1,0:T(8,128)(2,1)}), bf16[32,42,128]{2,1,0:T(8,128)(2,1)S(1)}, u32[]{:S(2)}, u32[]{:S(2)}) async-start(bf16[32,42,128]{2,1,0:T(8,128)(2,1)} %fusion.1), calls=%async_computation.3 | async-start | bytes 786432 | tf_op jit(solution)/shard_map/all_to_all | solution.py:290
  179.2 7.6 %collective-permute-start.7 = (bf16[1,2,64,2048]{3,2,1,0:T(8,128)(2,1)S(1)}, bf16[1,2,64,2048]{3,2,1,0:T(8,128)(2,1)S(1)}, u32[]{:S(2)}, u32[]{:S(2)}) collective-permute-start(bf16[1,2,64,2048]{3,2,1,0:T(8,128)(2,1)S(1)} %bitcast.114), channel_id=1, source_target_pairs={{64,0},{128,64},{192,128},{256,192},{320,256},{384,320},{448,384},... | collective-permute-start | bytes 1572872 | tf_op jit(solution)/shard_map/ppermute | solution.py:299
  186.8 20.1 %collective-permute-done.7 = bf16[1,2,64,2048]{3,2,1,0:T(8,128)(2,1)S(1)} collective-permute-done((bf16[1,2,64,2048]{3,2,1,0:T(8,128)(2,1)S(1)}, bf16[1,2,64,2048]{3,2,1,0:T(8,128)(2,1)S(1)}, u32[]{:S(2)}, u32[]{:S(2)}) %collective-permute-start.7) | collective-permute-done | bytes 524320 | tf_op jit(solution)/shard_map/ppermute | solution.py:299
  206.9 9.2 %all-to-all-done.3.terms_ref = bf16[32,42,128]{2,1,0:T(8,128)(2,1)S(1)} async-done(((bf16[32,42,128]{2,1,0:T(8,128)(2,1)}), bf16[32,42,128]{2,1,0:T(8,128)(2,1)S(1)}, u32[]{:S(2)}, u32[]{:S(2)}) %all-to-all-start.3) | async-done | bytes 344096 | tf_op jit(solution)/shard_map/all_to_all | solution.py:290
  217.5 0.8 copy.106
  (84 shorter events, 7.5 us)
Async XLA Ops:
  7.2 148.0 %copy-start = (bf16[1,2,64,2048]{3,2,1,0:T(8,128)(2,1)S(1)}, bf16[1,2,64,2048]{3,2,1,0:T(8,128)(2,1)}, u32[]{:S(2)}) copy-start(bf16[1,2,64,2048]{3,2,1,0:T(8,128)(2,1)} %param.8) | copy-start | bytes 1572868
  7.2 7.7 %copy-start.8 = (bf16[1,32,1536]{2,1,0:T(8,128)(2,1)S(1)}, bf16[1,32,1536]{2,1,0:T(8,128)(2,1)}, u32[]{:S(2)}) copy-start(bf16[1,32,1536]{2,1,0:T(8,128)(2,1)} %param.12) | copy-start | bytes 294916
  7.2 7.7 %slice-start = ((bf16[1,32,1536]{2,1,0:T(8,128)(2,1)}), bf16[1,32,512]{2,1,0:T(8,128)(2,1)S(1)}, s32[]{:S(2)}) async-start(bf16[1,32,1536]{2,1,0:T(8,128)(2,1)} %param.12), calls=%async_computation.6 | async-start | bytes 65536 | tf_op jit(solution)/shard_map/slice | solution.py:353
  7.2 8.0 %copy-start.6 = (bf16[1,2,64,1024]{3,2,1,0:T(8,128)(2,1)S(1)}, bf16[1,2,64,1024]{3,2,1,0:T(8,128)(2,1)}, u32[]{:S(2)}) copy-start(bf16[1,2,64,1024]{3,2,1,0:T(8,128)(2,1)} %param.9) | copy-start | bytes 786436
  8.2 7.2 %copy-start.9 = (bf16[1,32,128]{2,1,0:T(8,128)(2,1)S(1)}, bf16[1,32,128]{2,1,0:T(8,128)(2,1)}, u32[]{:S(2)}) copy-start(bf16[1,32,128]{2,1,0:T(8,128)(2,1)} %param.14) | copy-start | bytes 24580
  9.2 6.3 %copy-start.5 = (bf16[1,2,64,2048]{3,2,1,0:T(8,128)(2,1)S(1)}, bf16[1,2,64,2048]{3,2,1,0:T(8,128)(2,1)}, u32[]{:S(2)}) copy-start(bf16[1,2,64,2048]{3,2,1,0:T(8,128)(2,1)} %param.11) | copy-start | bytes 1572868
  9.9 14.6 %all-to-all-start = ((bf16[8,128,128]{2,1,0:T(8,128)(2,1)}), bf16[8,128,128]{2,1,0:T(8,128)(2,1)S(1)}, u32[]{:S(2)}, u32[]{:S(2)}) async-start(bf16[8,128,128]{2,1,0:T(8,128)(2,1)} %bitcast.5), calls=%async_computation | async-start | bytes 524288 | tf_op jit(solution)/shard_map/all_to_all | solution.py:290
  14.8 58.3 %all-gather.5.cloned.1.call-start = ((), (), s32[]{:S(2)}) async-start(), calls=%async_computation.4 | async-start | bytes 2359296 | tf_op jit(solution)/shard_map/all_gather | solution.py:367
  24.5 0.7 copy-start.4
  25.3 108.5 %all-gather.7.cloned.1.call-start = ((), (), s32[]{:S(2)}) async-start(), calls=%async_computation.5 | async-start | bytes 3833856 | tf_op jit(solution)/shard_map/all_gather | solution.py:380
  73.2 5.7 %collective-permute-start = (bf16[4,64,3456]{2,1,0:T(8,128)(2,1)S(1)}, bf16[4,64,3456]{2,1,0:T(8,128)(2,1)}, u32[]{:S(2)}, u32[]{:S(2)}) collective-permute-start(bf16[4,64,3456]{2,1,0:T(8,128)(2,1)S(1)} %all_to_all.20.own_ref), channel_id=1, source_target_pairs={{0,1},{1,0},{2,3},{3,2},{4,5},{5,4},{6,7},{7,6},{8,9},{9,8},{10,11... | collective-permute-start | bytes 5308424 | tf_op jit(solution)/shard_map/ppermute | solution.py:294
  110.7 17.8 %copy-start.7 = (bf16[1,64,1280]{2,1,0:T(8,128)(2,1)S(1)}, bf16[1,64,1280]{2,1,0:T(8,128)(2,1)}, u32[]{:S(2)}) copy-start(bf16[1,64,1280]{2,1,0:T(8,128)(2,1)} %param.15) | copy-start | bytes 491524
  110.7 12.2 %collective-permute-start.1 = (bf16[4,64,256]{2,1,0:T(8,128)(2,1)S(1)}, bf16[4,64,256]{2,1,0:T(8,128)(2,1)S(1)}, u32[]{:S(2)}, u32[]{:S(2)}) collective-permute-start(bf16[4,64,256]{2,1,0:T(8,128)(2,1)S(1)} %slice_bitcast_fusion.3), channel_id=1, source_target_pairs={{0,1},{1,0},{2,3},{3,2},{4,5},{5,4},{6,7},{7,6},{8,9},{9,8},{10,11... | collective-permute-start | bytes 393224 | tf_op jit(solution)/shard_map/ppermute | solution.py:294
  113.0 41.8 %all-to-all-start.2 = ((bf16[64,64,128]{2,1,0:T(8,128)(2,1)}), bf16[64,64,128]{2,1,0:T(8,128)(2,1)S(1)}, u32[]{:S(2)}, u32[]{:S(2)}) async-start(bf16[64,64,128]{2,1,0:T(8,128)(2,1)} %bitcast.28), calls=%async_computation.2 | async-start | bytes 2097152 | tf_op jit(solution)/shard_map/all_to_all | solution.py:290
  123.0 21.3 %collective-permute-start.2 = (bf16[2,64,256]{2,1,0:T(8,128)(2,1)S(1)}, bf16[2,64,256]{2,1,0:T(8,128)(2,1)S(1)}, u32[]{:S(2)}, u32[]{:S(2)}) collective-permute-start(bf16[2,64,256]{2,1,0:T(8,128)(2,1)S(1)} %get-tuple-element.53), channel_id=1, source_target_pairs={{0,48},{16,0},{32,16},{48,32},{1,49},{17,1},{33,17},{49,33},{2,50}... | collective-permute-start | bytes 196616 | tf_op jit(solution)/shard_map/ppermute | solution.py:303
  128.9 25.5 %collective-permute-start.3 = (bf16[2,64,256]{2,1,0:T(8,128)(2,1)S(1)}, bf16[2,64,256]{2,1,0:T(8,128)(2,1)S(1)}, u32[]{:S(2)}, u32[]{:S(2)}) collective-permute-start(bf16[2,64,256]{2,1,0:T(8,128)(2,1)S(1)} %get-tuple-element.54), channel_id=1, source_target_pairs={{0,32},{16,48},{32,0},{48,16},{1,33},{17,49},{33,1},{49,17},{2,34}... | collective-permute-start | bytes 196616 | tf_op jit(solution)/shard_map/ppermute | solution.py:303
  130.9 23.6 %collective-permute-start.4 = (bf16[2,64,256]{2,1,0:T(8,128)(2,1)S(1)}, bf16[2,64,256]{2,1,0:T(8,128)(2,1)S(1)}, u32[]{:S(2)}, u32[]{:S(2)}) collective-permute-start(bf16[2,64,256]{2,1,0:T(8,128)(2,1)S(1)} %get-tuple-element.55), channel_id=1, source_target_pairs={{0,16},{16,32},{32,48},{48,0},{1,17},{17,33},{33,49},{49,1},{2,18}... | collective-permute-start | bytes 196616 | tf_op jit(solution)/shard_map/ppermute | solution.py:303
  133.8 22.0 %collective-permute-start.5 = (bf16[8,4,32,1664]{3,2,1,0:T(8,128)(2,1)}, bf16[8,4,32,1664]{3,2,1,0:T(8,128)(2,1)}, u32[]{:S(2)}, u32[]{:S(2)}) collective-permute-start(bf16[8,4,32,1664]{3,2,1,0:T(8,128)(2,1)} %bitcast.108), channel_id=1, source_target_pairs={{0,1},{1,0},{2,3},{3,2},{4,5},{5,4},{6,7},{7,6},{8,9},{9,8},{10,11... | collective-permute-start | bytes 10223624 | tf_op jit(solution)/shard_map/ppermute | solution.py:294
  160.9 1.2 copy-start.2
  162.4 8.5 %collective-permute-start.6 = (f32[32,42,128]{2,0,1:T(8,128)S(1)}, f32[32,42,128]{2,0,1:T(8,128)S(1)}, u32[]{:S(2)}, u32[]{:S(2)}) collective-permute-start(f32[32,42,128]{2,0,1:T(8,128)S(1)} %bitcast.123), channel_id=1, source_target_pairs={{0,1},{1,0},{2,3},{3,2},{4,5},{5,4},{6,7},{7,6},{8,9},{9,8},{10,11... | collective-permute-start | bytes 2064392 | tf_op jit(solution)/shard_map/ppermute | solution.py:294
  164.5 2.0 copy-start.1
  166.5 4.5 %copy-start.3 = (f32[32,2,42,128]{3,2,1,0:T(8,128)S(1)}, f32[32,2,42,128]{3,2,1,0:T(8,128)}, u32[]{:S(2)}) copy-start(f32[32,2,42,128]{3,2,1,0:T(8,128)} %copy-done.2) | copy-start | bytes 4128772
  172.1 44.0 %all-to-all-start.3 = ((bf16[32,42,128]{2,1,0:T(8,128)(2,1)}), bf16[32,42,128]{2,1,0:T(8,128)(2,1)S(1)}, u32[]{:S(2)}, u32[]{:S(2)}) async-start(bf16[32,42,128]{2,1,0:T(8,128)(2,1)} %fusion.1), calls=%async_computation.3 | async-start | bytes 786432 | tf_op jit(solution)/shard_map/all_to_all | solution.py:290
  179.2 27.6 %collective-permute-start.7 = (bf16[1,2,64,2048]{3,2,1,0:T(8,128)(2,1)S(1)}, bf16[1,2,64,2048]{3,2,1,0:T(8,128)(2,1)S(1)}, u32[]{:S(2)}, u32[]{:S(2)}) collective-permute-start(bf16[1,2,64,2048]{3,2,1,0:T(8,128)(2,1)S(1)} %bitcast.114), channel_id=1, source_target_pairs={{64,0},{128,64},{192,128},{256,192},{320,256},{384,320},{448,384},... | collective-permute-start | bytes 1572872 | tf_op jit(solution)/shard_map/ppermute | solution.py:299
Sparse Core Ops, SparseCore 0:
  25.4 47.6 all-gather.4
  75.8 49.1 all-gather.6
